TPU v7x, 256 devices: a whole 4x4x8 slice. The times are simulated.
256 devices in a mesh: cp: 128 (over y, x_lo, z, core), kv: 2 (over x_hi).
Axes of the slice: x: 4 (x_hi: 2, x_lo: 2; x = x_hi * 2 + x_lo), y: 4, z: 8, core: 2. Of those that a mesh axis runs over, the one named last changes fastest.
Arguments:
- queries: bfloat16 [32768, 4096], P('cp', 'kv'), may hold values from -48 to 48, as said below
- keys: bfloat16 [32768, 1024], P('cp'), may hold values from -8 to 8, as said below
- values: bfloat16 [32768, 1024], P('cp'), may hold values from -6 to 6
- out_grad: bfloat16 [32768, 4096], P('cp', 'kv'), may hold values from -6 to 6
- block_position: int32 [128], replicated, may hold values from 0 to 127, each once
Outputs:
- attended: bfloat16 [32768, 4096], P('cp', 'kv')
- query_grad: bfloat16 [32768, 4096], P('cp', 'kv')
- key_grad: bfloat16 [32768, 1024], P('cp', 'kv')
- value_grad: bfloat16 [32768, 1024], P('cp', 'kv')
Inputs may be any that keep to these rules, and one draw needn't show every extreme that they name: `queries`: real values. `keys`: real values.
All inputs are finite; a program needn't handle non-finite values.
Results may differ from a plain program's by a relative error of at most 0.023.
Values may be sent and summed in bfloat16 or wider, within the bound.
No kernel may reach another device: no remote copies, remote signals or barrier semaphores. Data moves between devices by JAX's collectives and lax.ppermute only.
A program may use at most 128 MiB of HBM per device.

v0:
```python
import jax
import jax.numpy as jnp
from jax import lax
from jax.sharding import PartitionSpec as P

KVH = 8
HD = 128
ROUNDS = 2


masked_value = -1e30


def from_behind(block, axis, distance):
    devices = range(lax.axis_size(axis))
    route = [((i - distance) % len(devices), i) for i in devices]
    return lax.ppermute(block, axis, route)


def head_scores(query_heads, key_heads):
    return jnp.einsum(
        "qgkd,tkd->gkqt", query_heads, key_heads, preferred_element_type=jnp.float32
    ) * HD ** (-0.5)


def send_forward(stacked):
    arrived = []
    current = stacked
    for offset in range(ROUNDS):
        current = from_behind(current, "cp", 1)
        arrived.append(current)
    return jnp.concatenate(arrived, axis=1)


def send_back(parts_far):
    carried = jnp.zeros_like(parts_far[0])
    for offset in range(ROUNDS - 1, -1, -1):
        carried = from_behind(carried + parts_far[offset], "cp", -1)
    return carried


def on_device(queries, keys, values, out_grad, block_position):
    block_rows = queries.shape[0]
    groups = queries.shape[1] // (KVH * HD)
    key_width = keys.shape[1]
    root_scale = HD ** (-0.5)
    query_heads = queries.reshape(block_rows, groups, KVH, HD)
    grad_heads = out_grad.reshape(block_rows, groups, KVH, HD)
    own_keys = keys.reshape(block_rows, KVH, HD)
    own_values = values.reshape(block_rows, KVH, HD)
    cycle_size = lax.axis_size("cp")
    position = lax.axis_index("cp")
    indices = jnp.arange(cycle_size, dtype=jnp.int32)
    own_order = jnp.sum(jnp.where(indices == position, block_position, 0))
    sources = (position - jnp.arange(1, ROUNDS + 1, dtype=jnp.int32)) % cycle_size
    far_order = jnp.sum(
        jnp.where(indices[None, :] == sources[:, None], block_position[None, :], 0), axis=1
    )
    visible = jnp.repeat(far_order < own_order, block_rows)
    key_value = jnp.stack([keys, values])
    far_pair = send_forward(key_value)
    far_keys = far_pair[0].reshape(ROUNDS * block_rows, KVH, HD)
    far_values = far_pair[1].reshape(ROUNDS * block_rows, KVH, HD)
    causal = jnp.arange(block_rows)[:, None] >= jnp.arange(block_rows)[None, :]
    near_scores = jnp.where(causal, head_scores(query_heads, own_keys), masked_value)
    far_scores = jnp.where(visible, head_scores(query_heads, far_keys), masked_value)
    row_max = jnp.maximum(jnp.max(near_scores, axis=-1), jnp.max(far_scores, axis=-1))
    row_sum = jnp.sum(jnp.exp(near_scores - row_max[..., None]), axis=-1) + jnp.sum(
        jnp.exp(far_scores - row_max[..., None]), axis=-1
    )
    log_norm = row_max + jnp.log(row_sum)
    near_probs = jnp.exp(near_scores - log_norm[..., None])
    far_probs = jnp.exp(far_scores - log_norm[..., None])
    near_rounded = near_probs.astype(jnp.bfloat16)
    far_rounded = far_probs.astype(jnp.bfloat16)
    summed_out = jnp.einsum(
        "gkqt,tkd->qgkd", near_rounded, own_values, preferred_element_type=jnp.float32
    )
    summed_out = summed_out + jnp.einsum(
        "gkqt,tkd->qgkd", far_rounded, far_values, preferred_element_type=jnp.float32
    )
    attended = summed_out.astype(jnp.bfloat16)
    row_dot = jnp.sum(
        grad_heads.astype(jnp.float32) * attended.astype(jnp.float32), axis=-1
    ).transpose(1, 2, 0)

    def gradients(probs, rounded, key_heads, value_heads):
        grad_probs = jnp.einsum(
            "qgkd,tkd->gkqt", grad_heads, value_heads, preferred_element_type=jnp.float32
        )
        grad_scores = (probs * (grad_probs - row_dot[..., None]) * root_scale).astype(jnp.bfloat16)
        query_part = jnp.einsum(
            "gkqt,tkd->qgkd", grad_scores, key_heads, preferred_element_type=jnp.float32
        )
        key_part = jnp.einsum(
            "gkqt,qgkd->tkd", grad_scores, query_heads, preferred_element_type=jnp.float32
        )
        value_part = jnp.einsum(
            "gkqt,qgkd->tkd", rounded, grad_heads, preferred_element_type=jnp.float32
        )
        return (query_part, key_part, value_part)

    near_grads = gradients(near_probs, near_rounded, own_keys, own_values)
    far_grads = gradients(far_probs, far_rounded, far_keys, far_values)
    query_grad = (
        (near_grads[0] + far_grads[0]).astype(jnp.bfloat16).reshape(block_rows, groups * KVH * HD)
    )
    own_part = jnp.stack(
        [near_grads[1].reshape(block_rows, key_width), near_grads[2].reshape(block_rows, key_width)]
    )
    parts_far = jnp.stack(
        [
            far_grads[1].reshape(ROUNDS, block_rows, key_width),
            far_grads[2].reshape(ROUNDS, block_rows, key_width),
        ],
        axis=1,
    )
    grad_total = lax.psum_scatter(
        own_part + send_back(parts_far), "kv", scatter_dimension=2, tiled=True
    )
    grad_pair = grad_total.astype(jnp.bfloat16)
    return (attended.reshape(block_rows, groups * KVH * HD), query_grad, grad_pair[0], grad_pair[1])


def solution(mesh):
    placed = (P("cp", "kv"), P("cp", None), P("cp", None), P("cp", "kv"), P())
    return jax.shard_map(
        on_device,
        mesh=mesh,
        in_specs=placed,
        out_specs=(P("cp", "kv"), P("cp", "kv"), P("cp", "kv"), P("cp", "kv")),
        check_vma=False,
    )
```

profile of v0, /device:TPU:1, one launch (start us, length us, event | category | flops | bytes accessed | tf_op | source)
XLA Modules:
  0.0 196.6 jit_solution(13412125598661062912)
XLA Ops:
  10.9 3.0 %collective-permute-start = (bf16[2,256,1024]{1,2,0:T(8,128)(2,1)}, bf16[2,256,1024]{1,2,0:T(8,128)(2,1)}, u32[]{:S(2)}, u32[]{:S(2)}) collective-permute-start(bf16[2,256,1024]{1,2,0:T(8,128)(2,1)} %pad_maximum_fusion), channel_id=1, source_target_pairs={{254,0},{0,2},{2,4},{4,6},{6,8},{8,10},{10,12},{12,14},{14,16},{16... | collective-permute-start | bytes 3145736 | tf_op jit(solution)/shard_map/ppermute | solution.py:17
  14.6 11.4 %collective-permute-done = bf16[2,256,1024]{1,2,0:T(8,128)(2,1)} collective-permute-done((bf16[2,256,1024]{1,2,0:T(8,128)(2,1)}, bf16[2,256,1024]{1,2,0:T(8,128)(2,1)}, u32[]{:S(2)}, u32[]{:S(2)}) %collective-permute-start) | collective-permute-done | bytes 1048608 | tf_op jit(solution)/shard_map/ppermute | solution.py:17
  26.0 2.5 %collective-permute-start.1 = (bf16[2,256,1024]{1,2,0:T(8,128)(2,1)}, bf16[2,256,1024]{1,2,0:T(8,128)(2,1)}, u32[]{:S(2)}, u32[]{:S(2)}) collective-permute-start(bf16[2,256,1024]{1,2,0:T(8,128)(2,1)} %collective-permute-done), channel_id=1, source_target_pairs={{254,0},{0,2},{2,4},{4,6},{6,8},{8,10},{10,12},{12,14},{14,16},{16... | collective-permute-start | bytes 3145736 | tf_op jit(solution)/shard_map/ppermute | solution.py:17
  30.1 2.3 %copy.74 = bf16[256,2048]{0,1:T(8,128)(2,1)} copy(bf16[256,2048]{1,0:T(8,128)(2,1)} %param.8) | data formatting | bytes 2097152 | tf_op args[3]
  33.6 2.1 %constant_dynamic-update-slice_fusion.1 = bf16[2,512,1024]{1,2,0:T(8,128)(2,1)S(1)} fusion(bf16[2,256,1024]{1,2,0:T(8,128)(2,1)} %collective-permute-done), kind=kLoop, calls=%fused_computation.53 | loop fusion | bytes 2097152
  35.7 4.8 %collective-permute-done.1 = bf16[2,256,1024]{1,2,0:T(8,128)(2,1)} collective-permute-done((bf16[2,256,1024]{1,2,0:T(8,128)(2,1)}, bf16[2,256,1024]{1,2,0:T(8,128)(2,1)}, u32[]{:S(2)}, u32[]{:S(2)}) %collective-permute-start.1) | collective-permute-done | bytes 1048608 | tf_op jit(solution)/shard_map/ppermute | solution.py:17
  43.0 2.2 %bitcast_reduce_fusion = (f32[2,8,256]{2,0,1:T(2,128)S(1)}, f32[8,512,256,2]{2,1,3,0:T(8,128)S(1)}) fusion(pred[512]{0:T(512)(128)(4,1)S(1)} %reshape.65, bf16[512,8,128,1]{0,2,3,1:T(8,128)(2,1)S(1)} %bitcast.147, bf16[256,2,8,128]{3,2,1,0:T(8,128)(2,1)S(1)} %bitcast.144), kind=kOutput, calls=%fused_computation.6 | convolution fusion | flops 543158272 | bytes 10502656 | tf_op jit(solution)/shard_map/qgkd,tkd->gkqt/dot_general | solution.py:21
  45.2 2.0 %fusion.4 = f32[2,8,256]{2,0,1:T(2,128)S(1)} fusion(f32[8,512,256,2]{2,1,3,0:T(8,128)S(1)} %get-tuple-element.19, f32[2,8,256]{2,0,1:T(2,128)S(1)} %max.10, pred[512]{0:T(512)(128)(4,1)S(1)} %reshape.65), kind=kLoop, calls=%fused_computation.8 | loop fusion | flops 8384512 | bytes 8421888 | tf_op jit(solution)/shard_map/reduce_sum | solution.py:68
  49.3 1.8 convolution_bitcast_fusion
  51.1 2.5 %copy.93 = f32[512,8,128]{2,1,0:T(8,128)} copy(f32[512,8,128]{2,0,1:T(8,128)S(1)} %convolution_bitcast_fusion) | data formatting | bytes 4194304 | tf_op jit(solution)/shard_map/gkqt,qgkd->tkd/transpose | solution.py:98
  53.6 2.7 %stack_reshape.15 = f32[2,1,256,1024]{3,2,0,1:T(8,128)} reshape(f32[512,8,128]{2,1,0:T(8,128)} %copy.93) | data formatting | bytes 4194304 | tf_op jit(solution)/shard_map/stack;reshape | solution.py:111
  56.4 3.4 %fusion.27 = f32[8,2,256,128]{2,3,1,0:T(8,128)S(1)} fusion(bf16[256,8,128,1]{2,1,0,3:T(8,128)(2,1)S(1)} %bitcast.157, f32[8,256,256,2]{2,1,3,0:T(8,128)} %copy-done, f32[2,8,256]{2,0,1:T(2,128)S(1)} %bitcast.170, pred[256,256]{0,1:T(8,128)(4,1)S(1)} %iota_compare_fusion), kind=kOutput, calls=%fused_computation.45 | convolution fusion | flops 272629760 | bytes 6897664 | tf_op jit(solution)/shard_map/gkqt,tkd->qgkd/dot_general | solution.py:76
  59.8 6.9 %multiply_reduce_fusion = (f32[256,2,8]{0,1,2:T(2,128)S(1)}, bf16[256,2,8,128]{0,3,1,2:T(8,128)(2,1)}) fusion(bf16[256,2,8,128]{0,3,2,1:T(8,128)(2,1)S(1)} %bitcast.162, bf16[512,8,128,1]{0,2,3,1:T(8,128)(2,1)S(1)} %bitcast.166, f32[8,512,256,2]{2,1,3,0:T(8,128)} %copy-done.2, f32[2,8,256]{2,0,1:T(2,128)S(1)} %bitcast.171, pred[512]{0:T(512)(128)(4,1)S(1)} %reshape.65, ...), kind=kOutput, calls=%fused_computation.29 | convolution fusion | flops 548401152 | bytes 13664768 | tf_op jit(solution)/shard_map/gkqt,tkd->qgkd/dot_general | solution.py:79
  66.8 3.6 %fusion.2 = bf16[2,8,256,512]{2,3,0,1:T(8,128)(2,1)S(1)} fusion(f32[8,512,256,2]{2,1,3,0:T(8,128)S(1)} %bitcast.142, f32[2,8,256]{2,0,1:T(2,128)S(1)} %bitcast.177, f32[2,8,256]{2,0,1:T(2,128)S(1)} %bitcast.172, pred[512]{0:T(512)(128)(4,1)S(1)} %reshape.65, bf16[512,8,128,1]{0,2,3,1:T(8,128)(2,1)S(1)} %bitcast.167, bf16[256,2,8,128]{0,3,2,1:T(8,128)(2,1)S(1)} %bitcast.163), kind=kOutput, calls=%fused_computation.3 | convolution fusion | flops 551550976 | bytes 14713344 | tf_op jit(solution)/shard_map/qgkd,tkd->gkqt/dot_general | solution.py:88
  72.3 2.5 %copy.91 = f32[512,8,128]{2,1,0:T(8,128)} copy(f32[512,8,128]{2,0,1:T(8,128)S(1)} %convolution_bitcast_fusion.1) | data formatting | bytes 4194304 | tf_op jit(solution)/shard_map/gkqt,qgkd->tkd/transpose | solution.py:95
  74.9 2.7 %stack_reshape.14 = f32[2,1,256,1024]{3,2,0,1:T(8,128)} reshape(f32[512,8,128]{2,1,0:T(8,128)} %copy.91) | data formatting | bytes 4194304 | tf_op jit(solution)/shard_map/stack;reshape | solution.py:111
  77.6 1.9 constant_dynamic-update-slice_fusion.3
  80.3 12.2 %collective-permute-start.2 = (f32[2,256,1024]{2,1,0:T(8,128)S(1)}, f32[2,256,1024]{2,1,0:T(8,128)S(1)}, u32[]{:S(2)}, u32[]{:S(2)}) collective-permute-start(f32[2,256,1024]{2,1,0:T(8,128)S(1)} %slice_bitcast_fusion.1), channel_id=1, source_target_pairs={{2,0},{4,2},{6,4},{8,6},{10,8},{12,10},{14,12},{16,14},{18,16},{20... | collective-permute-start | bytes 6291464 | tf_op jit(solution)/shard_map/ppermute | solution.py:17
  92.5 14.1 %collective-permute-done.2 = f32[2,256,1024]{2,1,0:T(8,128)S(1)} collective-permute-done((f32[2,256,1024]{2,1,0:T(8,128)S(1)}, f32[2,256,1024]{2,1,0:T(8,128)S(1)}, u32[]{:S(2)}, u32[]{:S(2)}) %collective-permute-start.2) | collective-permute-done | bytes 2097184 | tf_op jit(solution)/shard_map/ppermute | solution.py:17
  106.6 1.7 fusion.12
  108.3 9.5 %collective-permute-start.3 = (f32[2,256,1024]{2,1,0:T(8,128)}, f32[2,256,1024]{2,1,0:T(8,128)}, u32[]{:S(2)}, u32[]{:S(2)}) collective-permute-start(f32[2,256,1024]{2,1,0:T(8,128)} %fusion.12), channel_id=1, source_target_pairs={{2,0},{4,2},{6,4},{8,6},{10,8},{12,10},{14,12},{16,14},{18,16},{20... | collective-permute-start | bytes 6291464 | tf_op jit(solution)/shard_map/ppermute | solution.py:17
  117.8 1.5 fusion.9
  119.3 1.8 fusion.15
  121.1 1.6 copy.88
  122.7 4.6 %fusion.23 = f32[8,256,128,1]{1,2,3,0:T(8,128)} fusion(bf16[256,2,8,128]{0,3,2,1:T(8,128)(2,1)} %bitcast.160, f32[8,256,256,2]{2,1,3,0:T(8,128)} %copy-done, f32[2,8,256]{2,0,1:T(2,128)S(1)} %bitcast.174, pred[256,256]{0,1:T(8,128)(4,1)S(1)} %iota_compare_fusion), kind=kOutput, calls=%fused_computation.41 | convolution fusion | flops 272629760 | bytes 6373376 | tf_op jit(solution)/shard_map/gkqt,qgkd->tkd/dot_general | solution.py:98
  127.3 2.5 %copy.89 = f32[1,256,1024]{2,1,0:T(8,128)} copy(f32[1,256,1024]{1,2,0:T(8,128)} %bitcast.165) | data formatting | bytes 2097152 | tf_op jit(solution)/shard_map/stack;reshape | solution.py:108
  129.8 4.3 %collective-permute-done.3 = f32[2,256,1024]{2,1,0:T(8,128)} collective-permute-done((f32[2,256,1024]{2,1,0:T(8,128)}, f32[2,256,1024]{2,1,0:T(8,128)}, u32[]{:S(2)}, u32[]{:S(2)}) %collective-permute-start.3) | collective-permute-done | bytes 2097184 | tf_op jit(solution)/shard_map/ppermute | solution.py:17
  134.1 3.8 %maximum_add_fusion = f32[2,256,1024]{2,1,0:T(8,128)} fusion(f32[2,256,1024]{2,1,0:T(8,128)} %collective-permute-done.3, f32[1,256,1024]{2,1,0:T(8,128)} %copy.89, f32[1,256,1024]{2,1,0:T(8,128)S(1)} %copy.88), kind=kLoop, calls=%fused_computation.24 | loop fusion | flops 1048576 | bytes 6291456 | tf_op jit(solution)/shard_map/add | solution.py:119
  137.9 2.2 %fusion.42 = f32[8,2,256,128]{2,3,1,0:T(8,128)S(1)} fusion(bf16[256,8,128,1]{0,2,3,1:T(8,128)(2,1)S(1)} %copy.106, bf16[2,8,256,256]{2,3,0,1:T(8,128)(2,1)} %copy-done.5), kind=kOutput, calls=%fused_computation.70 | convolution fusion | flops 268435456 | bytes 4718592 | tf_op jit(solution)/shard_map/gkqt,tkd->qgkd/dot_general | solution.py:92
  141.6 1.4 copy.96
  143.1 1.4 copy.95
  144.5 43.1 %reduce-scatter.2.cloned.1.call-done = f32[2,256,512]{2,1,0:T(8,128)} async-done(((f32[2,256,1024]{2,1,0:T(8,128)}), f32[2,256,512]{2,1,0:T(8,128)}) %reduce-scatter.2.cloned.1.call-update) | async-done | bytes 1048592 | tf_op jit(solution)/shard_map/reduce_scatter | solution.py:118
  (67 shorter events, 18.0 us)
Async XLA Ops:
  7.2 22.5 %copy-start.7 = (bf16[256,1024]{1,0:T(8,128)(2,1)S(1)}, bf16[256,1024]{1,0:T(8,128)(2,1)}, u32[]{:S(2)}) copy-start(bf16[256,1024]{1,0:T(8,128)(2,1)} %param.6) | copy-start | bytes 1572868
  7.2 6.8 %copy-start.15 = (s32[128]{0:T(128)S(1)}, s32[128]{0:T(128)}, u32[]{:S(2)}) copy-start(s32[128]{0:T(128)} %param.9) | copy-start | bytes 1540
  7.2 22.3 %copy-start.9 = (bf16[256,2048]{1,0:T(8,128)(2,1)S(1)}, bf16[256,2048]{1,0:T(8,128)(2,1)}, u32[]{:S(2)}) copy-start(bf16[256,2048]{1,0:T(8,128)(2,1)} %param.5) | copy-start | bytes 3145732
  7.2 180.4 %reduce-scatter.2.cloned.1.call-start = ((), (), s32[]{:S(2)}) async-start(), calls=%async_computation.1 | async-start | bytes 3145728 | tf_op jit(solution)/shard_map/reduce_scatter | solution.py:118
  9.8 22.5 %copy-start.8 = (bf16[256,1024]{1,0:T(8,128)(2,1)S(1)}, bf16[256,1024]{1,0:T(8,128)(2,1)}, u32[]{:S(2)}) copy-start(bf16[256,1024]{1,0:T(8,128)(2,1)} %param.7) | copy-start | bytes 1572868
  10.9 15.1 %collective-permute-start = (bf16[2,256,1024]{1,2,0:T(8,128)(2,1)}, bf16[2,256,1024]{1,2,0:T(8,128)(2,1)}, u32[]{:S(2)}, u32[]{:S(2)}) collective-permute-start(bf16[2,256,1024]{1,2,0:T(8,128)(2,1)} %pad_maximum_fusion), channel_id=1, source_target_pairs={{254,0},{0,2},{2,4},{4,6},{6,8},{8,10},{10,12},{12,14},{14,16},{16... | collective-permute-start | bytes 3145736 | tf_op jit(solution)/shard_map/ppermute | solution.py:17
  26.0 14.5 %collective-permute-start.1 = (bf16[2,256,1024]{1,2,0:T(8,128)(2,1)}, bf16[2,256,1024]{1,2,0:T(8,128)(2,1)}, u32[]{:S(2)}, u32[]{:S(2)}) collective-permute-start(bf16[2,256,1024]{1,2,0:T(8,128)(2,1)} %collective-permute-done), channel_id=1, source_target_pairs={{254,0},{0,2},{2,4},{4,6},{6,8},{8,10},{10,12},{12,14},{14,16},{16... | collective-permute-start | bytes 3145736 | tf_op jit(solution)/shard_map/ppermute | solution.py:17
  33.6 13.7 %copy-start = (f32[8,256,256,2]{2,1,3,0:T(8,128)}, f32[8,256,256,2]{2,1,3,0:T(8,128)S(1)}, u32[]{:S(2)}) copy-start(f32[8,256,256,2]{2,1,3,0:T(8,128)S(1)} %get-tuple-element.17) | copy-start | bytes 12582916
  45.2 3.2 %copy-start.2 = (f32[8,512,256,2]{2,1,3,0:T(8,128)}, f32[8,512,256,2]{2,1,3,0:T(8,128)S(1)}, u32[]{:S(2)}) copy-start(f32[8,512,256,2]{2,1,3,0:T(8,128)S(1)} %get-tuple-element.19) | copy-start | bytes 25165828
  47.3 2.0 %copy-start.10 = (bf16[256,2048]{0,1:T(8,128)(2,1)S(1)}, bf16[256,2048]{0,1:T(8,128)(2,1)}, u32[]{:S(2)}) copy-start(bf16[256,2048]{0,1:T(8,128)(2,1)} %copy.74) | copy-start | bytes 3145732
  56.4 3.5 %copy-start.11 = (bf16[256,2048]{0,1:T(8,128)(2,1)S(1)}, bf16[256,2048]{0,1:T(8,128)(2,1)}, u32[]{:S(2)}) copy-start(bf16[256,2048]{0,1:T(8,128)(2,1)} %copy.74) | copy-start | bytes 3145732
  56.4 3.5 %copy-start.14 = (bf16[1,512,1024]{1,2,0:T(8,128)(2,1)S(1)}, bf16[1,512,1024]{1,2,0:T(8,128)(2,1)}, u32[]{:S(2)}) copy-start(bf16[1,512,1024]{1,2,0:T(8,128)(2,1)} %get-tuple-element.12) | copy-start | bytes 3145732
  56.4 10.4 %slice-start = ((s8[8388608]{0:T(1024)(128)(4,1)}), s8[4194304]{0:T(1024)(128)(4,1)S(1)}, s32[]{:S(2)}) async-start(s8[8388608]{0:T(1024)(128)(4,1)} %bitcast.141), calls=%async_computation.2 | async-start | bytes 8388608
  59.8 6.9 %slice-start.1 = ((s8[8388608]{0:T(1024)(128)(4,1)}), s8[4194304]{0:T(1024)(128)(4,1)S(1)}, s32[]{:S(2)}) async-start(s8[8388608]{0:T(1024)(128)(4,1)} %bitcast.141), calls=%async_computation.3 | async-start | bytes 8388608
  70.4 1.9 copy-start.3
  77.6 2.2 %copy-start.6 = (f32[2,1,256,1024]{3,2,0,1:T(8,128)S(1)}, f32[2,1,256,1024]{3,2,0,1:T(8,128)}, u32[]{:S(2)}) copy-start(f32[2,1,256,1024]{3,2,0,1:T(8,128)} %stack_reshape.15) | copy-start | bytes 6291460
  80.3 37.5 %copy-start.1 = (f32[8,256,256,2]{2,1,3,0:T(8,128)S(1)}, f32[8,256,256,2]{2,1,3,0:T(8,128)}, u32[]{:S(2)}) copy-start(f32[8,256,256,2]{2,1,3,0:T(8,128)} %copy-done) | copy-start | bytes 12582916
  80.3 37.5 %copy-start.12 = (bf16[256,2048]{0,1:T(8,128)(2,1)S(1)}, bf16[256,2048]{0,1:T(8,128)(2,1)}, u32[]{:S(2)}) copy-start(bf16[256,2048]{0,1:T(8,128)(2,1)} %copy.74) | copy-start | bytes 3145732
  80.3 26.3 %collective-permute-start.2 = (f32[2,256,1024]{2,1,0:T(8,128)S(1)}, f32[2,256,1024]{2,1,0:T(8,128)S(1)}, u32[]{:S(2)}, u32[]{:S(2)}) collective-permute-start(f32[2,256,1024]{2,1,0:T(8,128)S(1)} %slice_bitcast_fusion.1), channel_id=1, source_target_pairs={{2,0},{4,2},{6,4},{8,6},{10,8},{12,10},{14,12},{16,14},{18,16},{20... | collective-permute-start | bytes 6291464 | tf_op jit(solution)/shard_map/ppermute | solution.py:17
  108.3 25.8 %collective-permute-start.3 = (f32[2,256,1024]{2,1,0:T(8,128)}, f32[2,256,1024]{2,1,0:T(8,128)}, u32[]{:S(2)}, u32[]{:S(2)}) collective-permute-start(f32[2,256,1024]{2,1,0:T(8,128)} %fusion.12), channel_id=1, source_target_pairs={{2,0},{4,2},{6,4},{8,6},{10,8},{12,10},{14,12},{16,14},{18,16},{20... | collective-permute-start | bytes 6291464 | tf_op jit(solution)/shard_map/ppermute | solution.py:17
  119.3 1.8 copy-start.5
  137.9 2.8 %copy-start.4 = (bf16[2,8,256,512]{2,3,0,1:T(8,128)(2,1)S(1)}, bf16[2,8,256,512]{2,3,0,1:T(8,128)(2,1)}, u32[]{:S(2)}) copy-start(bf16[2,8,256,512]{2,3,0,1:T(8,128)(2,1)} %copy-done.3) | copy-start | bytes 12582916
  141.5 1.5 copy-start.13
Sparse Core Ops, SparseCore 0:
  138.0 49.5 reduce-scatter.1
where the time goes:
time: 197 us
  waiting for transfers between devices  77.7 us (39%)
  local copies, waits for them, and re-layouts  33.7 us (17%)
  matrix products  31.2 us (16%)
  starting transfers between devices  27.2 us (14%)
  between operations  14.4 us (7%)
  other arithmetic  12.3 us (6%)
    reduce_scatter x1, waiting for transfers between devices, on_device(): lax.psum_scatter(own_part + send_back(parts_far), 'kv', scatter_dimension...  43.1 us
    ppermute x4, waiting for transfers between devices, from_behind(): return lax.ppermute(block, axis, route)  34.6 us
    ppermute x4, starting transfers between devices, from_behind(): return lax.ppermute(block, axis, route)  27.2 us
    unnamed x46, local copies, waits for them, and re-layouts  14.8 us
    dot_general x1, matrix products, on_device(): jnp.einsum('gkqt,tkd->qgkd', far_rounded, far_values, preferred_element_t...  6.9 us
    dot_general x2, matrix products, gradients(): jnp.einsum('gkqt,qgkd->tkd', rounded, grad_heads, preferred_element_type=...  6.44 us
    another operation x3, local copies, waits for them, and re-layouts, on_device(): jnp.stack([far_grads[1].reshape(ROUNDS, block_rows, key_width), far_grads...  5.68 us
    dot_general x2, matrix products, gradients(): jnp.einsum('qgkd,tkd->gkqt', grad_heads, value_heads, preferred_element_t...  5.11 us
  transfers between devices with their start and end apart: 5, of which 5 were waited for; matrix products, arithmetic and copies ran while one was open for 13% of the time, Pallas kernels for 0%

commit v1 on v0

v1 whole, which is shorter than its diff:
```python
import functools

import jax
import jax.numpy as jnp
from jax import lax
from jax.experimental import pallas as pl
from jax.experimental.pallas import tpu as pltpu
from jax.sharding import PartitionSpec as P

KVH = 8
HD = 128
ROUNDS = 2
CHUNKS = 2
LOG2E = 1.4426950408889634
MASKED = -1e30


def dot(left, right, left_dim, right_dim):
    dims = (((left_dim,), (right_dim,)), ((), ()))
    return lax.dot_general(left, right, dims, preferred_element_type=jnp.float32)


def attend(place, order, q0, q1, d0, d1, key, value, far1, far2, a0, a1, g0, g1, near, back1, back2):
    rows = key.shape[0]
    scale = HD**-0.5
    query = jnp.concatenate([q0[...], q1[...]], 0)
    grad = jnp.concatenate([d0[...], d1[...]], 0)
    keys = [key[...], far1[:rows, :], far2[:rows, :]]
    values = [value[...], far1[rows:, :], far2[rows:, :]]
    own = order[place[0]]
    seen = [order[place[r]] < own for r in range(1, ROUNDS + 1)]
    scores = [dot(k, query, 1, 1) for k in keys]
    key_row = lax.broadcasted_iota(jnp.int32, (rows, 2 * rows), 0)
    query_row = lax.broadcasted_iota(jnp.int32, (rows, 2 * rows), 1) % rows
    scores[0] = jnp.where(key_row <= query_row, scores[0], MASKED)
    top = jnp.max(scores[0], 0, keepdims=True)
    for s, visible in zip(scores[1:], seen):
        top = jnp.maximum(top, jnp.where(visible, jnp.max(s, 0, keepdims=True), MASKED))
    tops = [top] + [jnp.where(visible, top, -MASKED) for visible in seen]
    probs = [jnp.exp2((s - t) * (scale * LOG2E)) for s, t in zip(scores, tops)]
    inverse = 1.0 / sum(jnp.sum(p, 0, keepdims=True) for p in probs)
    probs = [p * inverse for p in probs]
    rounded = [p.astype(jnp.bfloat16) for p in probs]
    out = sum(dot(v, p, 0, 0) for v, p in zip(values, rounded))
    attended = out.T.astype(jnp.bfloat16)
    a0[...] = attended[:rows]
    a1[...] = attended[rows:]
    row_dot = jnp.sum(
        grad.T.astype(jnp.float32) * out.astype(jnp.bfloat16).astype(jnp.float32), 0, keepdims=True
    )
    query_grad = 0.0
    for k, v, p, r, ref in zip(keys, values, probs, rounded, (near, back1, back2)):
        ds = (p * (dot(v, grad, 1, 1) - row_dot)).astype(jnp.bfloat16)
        ref[:rows, :] = (dot(ds, query, 1, 0) * scale).astype(ref.dtype)
        ref[rows:, :] = dot(r, grad, 1, 0).astype(ref.dtype)
        query_grad = query_grad + dot(k, ds, 0, 0)
    query_grad = (query_grad * scale).T.astype(jnp.bfloat16)
    g0[...] = query_grad[:rows]
    g1[...] = query_grad[rows:]


def head_of(chunk, t):
    half = KVH // CHUNKS // 2
    return (t // half) * (KVH // 2) + chunk * half + t % half


def attend_chunk(chunk, place, order, queries, out_grad, keys, values, far1, far2):
    rows = keys.shape[0]
    heads = KVH // CHUNKS
    width = heads * HD
    smem = pl.BlockSpec(memory_space=pltpu.SMEM)
    first = pl.BlockSpec((rows, HD), lambda t: (0, head_of(chunk, t)))
    second = pl.BlockSpec((rows, HD), lambda t: (0, head_of(chunk, t) + KVH))
    single = pl.BlockSpec((rows, HD), lambda t: (0, t))
    double = pl.BlockSpec((2 * rows, HD), lambda t: (0, t))
    flops = 6 * 2 * heads * (2 * rows) * (3 * rows) * HD
    return pl.pallas_call(
        attend,
        grid=(heads,),
        in_specs=[smem, smem, first, second, first, second, first, first, double, double],
        out_specs=[single] * 4 + [double] * 3,
        out_shape=[jax.ShapeDtypeStruct((rows, width), jnp.bfloat16)] * 4
        + [jax.ShapeDtypeStruct((2 * rows, width), jnp.float32)]
        + [jax.ShapeDtypeStruct((2 * rows, width), jnp.bfloat16)] * 2,
        compiler_params=pltpu.CompilerParams(vmem_limit_bytes=32 * 2**20),
        cost_estimate=pl.CostEstimate(
            flops=flops, bytes_accessed=12 * rows * width * 2, transcendentals=heads * 6 * rows * rows
        ),
    )(place, order, queries, queries, out_grad, out_grad, keys, values, far1, far2)


def columns(x, chunk):
    half = KVH // CHUNKS // 2 * HD
    middle = x.shape[1] // 2
    return jnp.concatenate(
        [x[:, chunk * half : (chunk + 1) * half], x[:, middle + chunk * half : middle + (chunk + 1) * half]], 1
    )


def on_device(queries, keys, values, out_grad, block_position):
    size = lax.axis_size("cp")
    position = lax.axis_index("cp")
    core = position % 2
    side = lax.axis_index("kv")
    place = (position - jnp.arange(ROUNDS + 1, dtype=jnp.int32)) % size
    ahead = [(i, (i + 2) % size) for i in range(size)]
    behind = [((i + 2) % size, i) for i in range(size)]
    swap = [(i, i ^ 1) for i in range(size)]
    across = [(0, 1), (1, 0)]
    bf16, f32 = jnp.bfloat16, jnp.float32
    rows = keys.shape[0]

    own = [jnp.concatenate([columns(keys, c), columns(values, c)], 0) for c in range(CHUNKS)]
    far2, far1 = [], []
    for c in range(CHUNKS):
        x = own[c]
        if c:
            x, _ = lax.optimization_barrier((x, far2[-1]))
        far2.append(lax.ppermute(x, "cp", ahead))
    for c in range(CHUNKS):
        far1.append(lax.ppermute(jnp.where(core == 0, own[c], far2[c]), "cp", swap))
    parts = []
    total = []
    for c in range(CHUNKS):
        a0, a1, g0, g1, near, back1, back2 = attend_chunk(
            c, place, block_position, queries, out_grad, keys, values, far1[c], far2[c]
        )
        parts.append((a0, a1, g0, g1))
        got = lax.ppermute(back1, "cp", swap)
        zero = jnp.zeros((), f32)
        got = got.astype(f32)
        summed = (back2.astype(f32) + jnp.where(core == 1, got, zero)).astype(bf16)
        arrived = lax.ppermute(summed, "cp", behind)
        mine = near + jnp.where(core == 0, got, zero) + arrived.astype(f32)
        half = mine.shape[1] // 2
        give = jnp.where(side == 0, mine[:, half:], mine[:, :half]).astype(bf16)
        keep = jnp.where(side == 0, mine[:, :half], mine[:, half:])
        total.append((keep + lax.ppermute(give, "kv", across).astype(f32)).astype(bf16))

    def join(index):
        halves = KVH // CHUNKS // 2 * HD
        pieces = []
        for g in (0, 1):
            for h in (0, 1):
                pieces += [p[index + g][:, h * halves : (h + 1) * halves] for p in parts]
        return jnp.concatenate(pieces, 1)

    key_grad = jnp.concatenate([t[:rows] for t in total], 1)
    value_grad = jnp.concatenate([t[rows:] for t in total], 1)
    return join(0), join(2), key_grad, value_grad


def solution(mesh):
    placed = (P("cp", "kv"), P("cp", None), P("cp", None), P("cp", "kv"), P())
    return jax.shard_map(
        on_device,
        mesh=mesh,
        in_specs=placed,
        out_specs=(P("cp", "kv"), P("cp", "kv"), P("cp", "kv"), P("cp", "kv")),
        check_vma=False,
    )
```

time: 197 us -> 82.2 us (0.42)
  waiting for transfers between devices: 77.7 us -> 44.1 us
  matrix products: 31.2 us -> 0 us
  local copies, waits for them, and re-layouts: 33.7 us -> 2.84 us
  Pallas kernels: 0 us -> 18.7 us
  starting transfers between devices: 27.2 us -> 10.8 us
  between operations: 14.4 us -> 0.92 us
  other arithmetic: 12.3 us -> 4.42 us
    reduce_scatter x1 -> x0, waiting for transfers between devices: 43.1 us -> none  [on_device(): lax.psum_scatter(own_part + send_back(parts_far), 'kv', scatter_dimension...]
    dot_general x12 -> x0, matrix products: 31.2 us -> none  [the longest x1 6.9 us: on_device(): jnp.einsum('gkqt,tkd->qgkd', far_rounded, far_values, preferred_element_t...]
    pallas_call x0 -> x2, Pallas kernels: none -> 18.7 us  [attend_chunk(): pl.pallas_call(attend, grid=(heads,), in_specs=[smem, smem, first, second...]
    ppermute x4 -> x10, starting transfers between devices: 27.2 us -> 10.8 us  [the longest x2 5.07 us: on_device(): lax.ppermute(give, 'kv', across).astype(f32)]
    unnamed x46 -> x32, local copies, waits for them, and re-layouts: 14.8 us -> 1.41 us
    another operation x5 -> x0, local copies, waits for them, and re-layouts: 9.76 us -> none  [the longest x3 5.68 us: on_device(): jnp.stack([far_grads[1].reshape(ROUNDS, block_rows, key_width), far_grads...]
    ppermute x4 -> x10, waiting for transfers between devices: 34.6 us -> 44.1 us  [the longest x2 24.7 us: on_device(): far2.append(lax.ppermute(x, 'cp', ahead))]
    transpose x2 -> x0, local copies, waits for them, and re-layouts: 5.07 us -> none  [the longest x1 2.54 us: gradients(): jnp.einsum('gkqt,qgkd->tkd', grad_scores, query_heads, preferred_element_...]
  transfers between devices with their start and end apart: 5 -> 10, of which waited for: 5 -> 8; matrix products, arithmetic and copies ran while one was open for 13% -> 3% of each run, Pallas kernels for 0% -> 23%
where the time goes in v1:
time: 82.2 us; the launch traced here: 81.7 us
  waiting for transfers between devices  44.1 us (54%)
  Pallas kernels  18.7 us (23%)
  starting transfers between devices  10.8 us (13%)
  other arithmetic  4.42 us (5%)
  local copies, waits for them, and re-layouts  2.84 us (3%)
  between operations  0.92 us (1%)
    ppermute x2, waiting for transfers between devices, on_device(): far2.append(lax.ppermute(x, 'cp', ahead))  24.7 us
    pallas_call x2, Pallas kernels, attend_chunk(): pl.pallas_call(attend, grid=(heads,), in_specs=[smem, smem, first, second...  18.7 us
    ppermute x2, waiting for transfers between devices, on_device(): arrived = lax.ppermute(summed, 'cp', behind)  10.3 us
    ppermute x2, waiting for transfers between devices, on_device(): lax.ppermute(give, 'kv', across).astype(f32)  5.52 us
    ppermute x2, starting transfers between devices, on_device(): lax.ppermute(give, 'kv', across).astype(f32)  5.07 us
    ppermute x2, starting transfers between devices, on_device(): far2.append(lax.ppermute(x, 'cp', ahead))  2.55 us
    ppermute x2, waiting for transfers between devices, on_device(): far1.append(lax.ppermute(jnp.where(core == 0, own[c], far2[c]), 'cp', swap))  2.26 us
    ppermute x2, starting transfers between devices, on_device(): far1.append(lax.ppermute(jnp.where(core == 0, own[c], far2[c]), 'cp', swap))  2.11 us
  transfers between devices with their start and end apart: 10, of which 8 were waited for; matrix products, arithmetic and copies ran while one was open for 3% of the time, Pallas kernels for 23%

profile of v1, /device:TPU:1, one launch (start us, length us, event | category | flops | bytes accessed | tf_op | source)
XLA Modules:
  0.0 81.7 jit_solution(3611925268462325798)
XLA Ops:
  0.6 1.4 %fusion.9 = (bf16[256,256]{1,0:T(8,128)(2,1)S(1)}, bf16[256,256]{1,0:T(8,128)(2,1)S(1)}, bf16[256,256]{1,0:T(8,128)(2,1)S(1)}, bf16[256,256]{1,0:T(8,128)(2,1)S(...) fusion(bf16[256,1024]{1,0:T(8,128)(2,1)} %key.3, ...), kind=kLoop, calls=%fused_computation.42 | loop fusion | bytes 2097152 | tf_op jit(solution)/shard_map/slice | solution.py:96
  2.1 2.5 %collective-permute-start = (bf16[512,512]{1,0:T(8,128)(2,1)S(1)}, bf16[512,512]{1,0:T(8,128)(2,1)S(1)}, u32[]{:S(2)}, u32[]{:S(2)}) collective-permute-start(bf16[512,512]{1,0:T(8,128)(2,1)S(1)} %maximum_maximum_fusion), channel_id=1, source_target_pairs={{0,4},{2,6},{4,8},{6,10},{8,12},{10,14},{12,16},{14,18},{16,20},{1... | collective-permute-start | bytes 1572872 | tf_op jit(solution)/shard_map/ppermute | solution.py:119
  4.6 19.0 %collective-permute-done.far2 = bf16[512,512]{1,0:T(8,128)(2,1)S(1)} collective-permute-done((bf16[512,512]{1,0:T(8,128)(2,1)S(1)}, bf16[512,512]{1,0:T(8,128)(2,1)S(1)}, u32[]{:S(2)}, u32[]{:S(2)}) %collective-permute-start) | collective-permute-done | bytes 524320 | tf_op jit(solution)/shard_map/ppermute | solution.py:119
  23.6 0.9 %broadcast_select_fusion.1 = bf16[512,512]{1,0:T(8,128)(2,1)} fusion(bf16[512,512]{1,0:T(8,128)(2,1)S(1)} %collective-permute-done.far2, pred[]{:T(512)S(6)} %eq.10, bf16[256,256]{1,0:T(8,128)(2,1)S(1)} %get-tuple-element.48, bf16[256,256]{1,0:T(8,128)(2,1)S(1)} %get-tuple-element.47, bf16[256,256]{1,0:T(8,128)(2,1)S(1)} %get-tuple-element.35, ...), kind=kLoop, calls=%fused_computation.19 | loop fusion | flops 2359296 | bytes 1572865 | tf_op jit(solution)/shard_map/jit(_where)/select_n | solution.py:121
  24.5 1.2 %collective-permute-start.1 = (bf16[512,512]{1,0:T(8,128)(2,1)}, bf16[512,512]{1,0:T(8,128)(2,1)}, u32[]{:S(2)}, u32[]{:S(2)}) collective-permute-start(bf16[512,512]{1,0:T(8,128)(2,1)} %broadcast_select_fusion.1), channel_id=1, source_target_pairs={{0,2},{2,0},{4,6},{6,4},{8,10},{10,8},{12,14},{14,12},{16,18},{18,... | collective-permute-start | bytes 1572872 | tf_op jit(solution)/shard_map/ppermute | solution.py:121
  25.7 0.8 %maximum_maximum_fusion.1 = bf16[512,512]{1,0:T(8,128)(2,1)} fusion(bf16[256,256]{1,0:T(8,128)(2,1)S(1)} %get-tuple-element.46, bf16[256,256]{1,0:T(8,128)(2,1)S(1)} %get-tuple-element.49, bf16[256,256]{1,0:T(8,128)(2,1)S(1)} %get-tuple-element.37, bf16[256,256]{1,0:T(8,128)(2,1)S(1)} %get-tuple-element.34), kind=kLoop, calls=%fused_computation.13 | loop fusion | flops 2097152 | bytes 1048576 | tf_op jit(solution)/shard_map/concatenate | solution.py:113
  26.6 1.0 %collective-permute-done.1.far1 = bf16[512,512]{1,0:T(8,128)(2,1)} collective-permute-done((bf16[512,512]{1,0:T(8,128)(2,1)}, bf16[512,512]{1,0:T(8,128)(2,1)}, u32[]{:S(2)}, u32[]{:S(2)}) %collective-permute-start.1) | collective-permute-done | bytes 524320 | tf_op jit(solution)/shard_map/ppermute | solution.py:121
  27.6 1.2 %copy-done.3 = bf16[256,2048]{1,0:T(8,128)(2,1)S(1)} copy-done((bf16[256,2048]{1,0:T(8,128)(2,1)S(1)}, bf16[256,2048]{1,0:T(8,128)(2,1)}, u32[]{:S(2)}) %copy-start.3) | copy-done | bytes 1048600
  28.8 9.5 %shard_map.84 = (bf16[256,512]{1,0:T(8,128)(2,1)S(1)}, bf16[256,512]{1,0:T(8,128)(2,1)S(1)}, bf16[256,512]{1,0:T(8,128)(2,1)S(1)}, bf16[256,512]{1,0:T(8,128)(2,...) custom-call(s32[3]{0:T(128)S(1)} %and_select_fusion.place, ...), custom_call_target="tpu_custom_call" | custom-call | flops 2415919104 | bytes 3145728 | tf_op jit(solution)/shard_map/pallas_call | solution.py:77
  38.3 0.5 collective-permute-start.4
  38.8 5.8 %collective-permute-done.2.far2 = bf16[512,512]{1,0:T(8,128)(2,1)S(1)} collective-permute-done((bf16[512,512]{1,0:T(8,128)(2,1)}, bf16[512,512]{1,0:T(8,128)(2,1)S(1)}, u32[]{:S(2)}, u32[]{:S(2)}) %collective-permute-start.2) | collective-permute-done | bytes 524320 | tf_op jit(solution)/shard_map/ppermute | solution.py:119
  44.5 0.1 broadcast_select_fusion
  44.7 0.9 %collective-permute-start.3 = (bf16[512,512]{1,0:T(8,128)(2,1)S(1)}, bf16[512,512]{1,0:T(8,128)(2,1)S(1)}, u32[]{:S(2)}, u32[]{:S(2)}) collective-permute-start(bf16[512,512]{1,0:T(8,128)(2,1)S(1)} %broadcast_select_fusion), channel_id=1, source_target_pairs={{0,2},{2,0},{4,6},{6,4},{8,10},{10,8},{12,14},{14,12},{16,18},{18,... | collective-permute-start | bytes 1572872 | tf_op jit(solution)/shard_map/ppermute | solution.py:121
  45.6 0.2 fusion.3
  45.8 0.1 collective-permute-start.5
  45.8 1.2 %collective-permute-done.3.far1 = bf16[512,512]{1,0:T(8,128)(2,1)S(1)} collective-permute-done((bf16[512,512]{1,0:T(8,128)(2,1)S(1)}, bf16[512,512]{1,0:T(8,128)(2,1)S(1)}, u32[]{:S(2)}, u32[]{:S(2)}) %collective-permute-start.3) | collective-permute-done | bytes 524320 | tf_op jit(solution)/shard_map/ppermute | solution.py:121
  47.1 9.2 %shard_map.85 = (bf16[256,512]{1,0:T(8,128)(2,1)S(1)}, bf16[256,512]{1,0:T(8,128)(2,1)S(1)}, bf16[256,512]{1,0:T(8,128)(2,1)S(1)}, bf16[256,512]{1,0:T(8,128)(2,...) custom-call(s32[3]{0:T(128)S(1)} %and_select_fusion.place, ...), custom_call_target="tpu_custom_call" | custom-call | flops 2415919104 | bytes 3145728 | tf_op jit(solution)/shard_map/pallas_call | solution.py:77
  56.3 0.5 collective-permute-start.7
  57.0 1.3 %collective-permute-done.7 = bf16[512,512]{1,0:T(8,128)(2,1)S(1)} collective-permute-done((bf16[512,512]{1,0:T(8,128)(2,1)S(1)}, bf16[512,512]{1,0:T(8,128)(2,1)S(1)}, u32[]{:S(2)}, u32[]{:S(2)}) %collective-permute-start.7) | collective-permute-done | bytes 524320 | tf_op jit(solution)/shard_map/ppermute | solution.py:129
  58.3 0.2 fusion.7
  58.5 0.1 collective-permute-start.8
  58.6 0.8 collective-permute-done.5
  59.4 0.2 fusion.1
  59.7 2.5 %collective-permute-start.6 = (bf16[512,256]{1,0:T(8,128)(2,1)S(1)}, bf16[512,256]{1,0:T(8,128)(2,1)S(1)}, u32[]{:S(2)}, u32[]{:S(2)}) collective-permute-start(bf16[512,256]{1,0:T(8,128)(2,1)S(1)} %select_convert_fusion.1), channel_id=1, source_target_pairs={{0,1},{1,0},{2,3},{3,2},{4,5},{5,4},{6,7},{7,6},{8,9},{9,8},{10,11... | collective-permute-start | bytes 786440 | tf_op jit(solution)/shard_map/ppermute | solution.py:138
  62.2 9.5 %collective-permute-done.8 = bf16[512,512]{1,0:T(8,128)(2,1)S(1)} collective-permute-done((bf16[512,512]{1,0:T(8,128)(2,1)S(1)}, bf16[512,512]{1,0:T(8,128)(2,1)S(1)}, u32[]{:S(2)}, u32[]{:S(2)}) %collective-permute-start.8) | collective-permute-done | bytes 524320 | tf_op jit(solution)/shard_map/ppermute | solution.py:133
  71.7 0.2 fusion.5
  72.0 2.5 %collective-permute-start.9 = (bf16[512,256]{1,0:T(8,128)(2,1)S(1)}, bf16[512,256]{1,0:T(8,128)(2,1)S(1)}, u32[]{:S(2)}, u32[]{:S(2)}) collective-permute-start(bf16[512,256]{1,0:T(8,128)(2,1)S(1)} %select_convert_fusion), channel_id=1, source_target_pairs={{0,1},{1,0},{2,3},{3,2},{4,5},{5,4},{6,7},{7,6},{8,9},{9,8},{10,11... | collective-permute-start | bytes 786440 | tf_op jit(solution)/shard_map/ppermute | solution.py:138
  74.5 0.1 add_convert_fusion.1
  74.7 5.5 %collective-permute-done.9 = bf16[512,256]{1,0:T(8,128)(2,1)S(1)} collective-permute-done((bf16[512,256]{1,0:T(8,128)(2,1)S(1)}, bf16[512,256]{1,0:T(8,128)(2,1)S(1)}, u32[]{:S(2)}, u32[]{:S(2)}) %collective-permute-start.9) | collective-permute-done | bytes 262176 | tf_op jit(solution)/shard_map/ppermute | solution.py:138
  80.2 0.1 add_convert_fusion
  80.3 0.7 pad_maximum_fusion.1
  81.0 0.7 pad_maximum_fusion
  (42 shorter events, 0.4 us)
Async XLA Ops:
  2.0 23.7 %copy-start.5 = (bf16[256,256]{1,0:T(8,128)(2,1)}, bf16[256,256]{1,0:T(8,128)(2,1)S(1)}, u32[]{:S(2)}) copy-start(bf16[256,256]{1,0:T(8,128)(2,1)S(1)} %get-tuple-element.49) | copy-start | bytes 393220
  2.1 21.5 %collective-permute-start = (bf16[512,512]{1,0:T(8,128)(2,1)S(1)}, bf16[512,512]{1,0:T(8,128)(2,1)S(1)}, u32[]{:S(2)}, u32[]{:S(2)}) collective-permute-start(bf16[512,512]{1,0:T(8,128)(2,1)S(1)} %maximum_maximum_fusion), channel_id=1, source_target_pairs={{0,4},{2,6},{4,8},{6,10},{8,12},{10,14},{12,16},{14,18},{16,20},{1... | collective-permute-start | bytes 1572872 | tf_op jit(solution)/shard_map/ppermute | solution.py:119
  4.6 23.0 %copy-start.2 = (bf16[256,2048]{1,0:T(8,128)(2,1)S(1)}, bf16[256,2048]{1,0:T(8,128)(2,1)}, u32[]{:S(2)}) copy-start(bf16[256,2048]{1,0:T(8,128)(2,1)} %q1.3) | copy-start | bytes 3145732
  24.5 3.1 %collective-permute-start.1 = (bf16[512,512]{1,0:T(8,128)(2,1)}, bf16[512,512]{1,0:T(8,128)(2,1)}, u32[]{:S(2)}, u32[]{:S(2)}) collective-permute-start(bf16[512,512]{1,0:T(8,128)(2,1)} %broadcast_select_fusion.1), channel_id=1, source_target_pairs={{0,2},{2,0},{4,6},{6,4},{8,10},{10,8},{12,14},{14,12},{16,18},{18,... | collective-permute-start | bytes 1572872 | tf_op jit(solution)/shard_map/ppermute | solution.py:121
  25.7 1.9 %copy-start = (bf16[256,1024]{1,0:T(8,128)(2,1)S(1)}, bf16[256,1024]{1,0:T(8,128)(2,1)}, u32[]{:S(2)}) copy-start(bf16[256,1024]{1,0:T(8,128)(2,1)} %key.3) | copy-start | bytes 1572868
  25.7 1.9 %copy-start.1 = (bf16[256,1024]{1,0:T(8,128)(2,1)S(1)}, bf16[256,1024]{1,0:T(8,128)(2,1)}, u32[]{:S(2)}) copy-start(bf16[256,1024]{1,0:T(8,128)(2,1)} %value.3) | copy-start | bytes 1572868
  26.6 18.0 %collective-permute-start.2 = (bf16[512,512]{1,0:T(8,128)(2,1)}, bf16[512,512]{1,0:T(8,128)(2,1)S(1)}, u32[]{:S(2)}, u32[]{:S(2)}) collective-permute-start(bf16[512,512]{1,0:T(8,128)(2,1)} %maximum_maximum_fusion.1), channel_id=1, source_target_pairs={{0,4},{2,6},{4,8},{6,10},{8,12},{10,14},{12,16},{14,18},{16,20},{1... | collective-permute-start | bytes 1572872 | tf_op jit(solution)/shard_map/ppermute | solution.py:119
  26.6 1.0 %copy-start.4 = (s32[128]{0:T(128)S(1)}, s32[128]{0:T(128)}, u32[]{:S(2)}) copy-start(s32[128]{0:T(128)} %order.3) | copy-start | bytes 1540
  27.6 1.2 %copy-start.3 = (bf16[256,2048]{1,0:T(8,128)(2,1)S(1)}, bf16[256,2048]{1,0:T(8,128)(2,1)}, u32[]{:S(2)}) copy-start(bf16[256,2048]{1,0:T(8,128)(2,1)} %d1.3) | copy-start | bytes 3145732
  28.8 15.7 %copy-start.6 = (bf16[256,256]{1,0:T(8,128)(2,1)S(1)}, bf16[256,256]{1,0:T(8,128)(2,1)}, u32[]{:S(2)}) copy-start(bf16[256,256]{1,0:T(8,128)(2,1)} %copy-done.5) | copy-start | bytes 393220
  38.3 7.3 %collective-permute-start.4 = (bf16[512,512]{1,0:T(8,128)(2,1)S(1)}, bf16[512,512]{1,0:T(8,128)(2,1)S(1)}, u32[]{:S(2)}, u32[]{:S(2)}) collective-permute-start(bf16[512,512]{1,0:T(8,128)(2,1)S(1)} %get-tuple-element.29), channel_id=1, source_target_pairs={{0,2},{2,0},{4,6},{6,4},{8,10},{10,8},{12,14},{14,12},{16,18},{18,... | collective-permute-start | bytes 1572872 | tf_op jit(solution)/shard_map/ppermute | solution.py:129
  44.7 2.4 %collective-permute-start.3 = (bf16[512,512]{1,0:T(8,128)(2,1)S(1)}, bf16[512,512]{1,0:T(8,128)(2,1)S(1)}, u32[]{:S(2)}, u32[]{:S(2)}) collective-permute-start(bf16[512,512]{1,0:T(8,128)(2,1)S(1)} %broadcast_select_fusion), channel_id=1, source_target_pairs={{0,2},{2,0},{4,6},{6,4},{8,10},{10,8},{12,14},{14,12},{16,18},{18,... | collective-permute-start | bytes 1572872 | tf_op jit(solution)/shard_map/ppermute | solution.py:121
  45.8 13.6 %collective-permute-start.5 = (bf16[512,512]{1,0:T(8,128)(2,1)S(1)}, bf16[512,512]{1,0:T(8,128)(2,1)S(1)}, u32[]{:S(2)}, u32[]{:S(2)}) collective-permute-start(bf16[512,512]{1,0:T(8,128)(2,1)S(1)} %fusion.3), channel_id=1, source_target_pairs={{4,0},{6,2},{8,4},{10,6},{12,8},{14,10},{16,12},{18,14},{20,16},{2... | collective-permute-start | bytes 1572872 | tf_op jit(solution)/shard_map/ppermute | solution.py:133
  56.3 2.0 %collective-permute-start.7 = (bf16[512,512]{1,0:T(8,128)(2,1)S(1)}, bf16[512,512]{1,0:T(8,128)(2,1)S(1)}, u32[]{:S(2)}, u32[]{:S(2)}) collective-permute-start(bf16[512,512]{1,0:T(8,128)(2,1)S(1)} %get-tuple-element.32), channel_id=1, source_target_pairs={{0,2},{2,0},{4,6},{6,4},{8,10},{10,8},{12,14},{14,12},{16,18},{18,... | collective-permute-start | bytes 1572872 | tf_op jit(solution)/shard_map/ppermute | solution.py:129
  56.9 1.6 %copy-start.8 = (bf16[256,2048]{1,0:T(8,128)(2,1)}, bf16[256,2048]{1,0:T(8,128)(2,1)S(1)}, u32[]{:S(2)}) copy-start(bf16[256,2048]{1,0:T(8,128)(2,1)S(1)} %slice_dynamic-update-slice_fusion) | copy-start | bytes 3145732
  57.0 2.6 %copy-start.7 = (bf16[256,2048]{1,0:T(8,128)(2,1)}, bf16[256,2048]{1,0:T(8,128)(2,1)S(1)}, u32[]{:S(2)}) copy-start(bf16[256,2048]{1,0:T(8,128)(2,1)S(1)} %slice_dynamic-update-slice_fusion.8) | copy-start | bytes 3145732
  58.5 13.2 %collective-permute-start.8 = (bf16[512,512]{1,0:T(8,128)(2,1)S(1)}, bf16[512,512]{1,0:T(8,128)(2,1)S(1)}, u32[]{:S(2)}, u32[]{:S(2)}) collective-permute-start(bf16[512,512]{1,0:T(8,128)(2,1)S(1)} %fusion.7), channel_id=1, source_target_pairs={{4,0},{6,2},{8,4},{10,6},{12,8},{14,10},{16,12},{18,14},{20,16},{2... | collective-permute-start | bytes 1572872 | tf_op jit(solution)/shard_map/ppermute | solution.py:133
  59.7 14.9 %collective-permute-start.6 = (bf16[512,256]{1,0:T(8,128)(2,1)S(1)}, bf16[512,256]{1,0:T(8,128)(2,1)S(1)}, u32[]{:S(2)}, u32[]{:S(2)}) collective-permute-start(bf16[512,256]{1,0:T(8,128)(2,1)S(1)} %select_convert_fusion.1), channel_id=1, source_target_pairs={{0,1},{1,0},{2,3},{3,2},{4,5},{5,4},{6,7},{7,6},{8,9},{9,8},{10,11... | collective-permute-start | bytes 786440 | tf_op jit(solution)/shard_map/ppermute | solution.py:138
  72.0 8.2 %collective-permute-start.9 = (bf16[512,256]{1,0:T(8,128)(2,1)S(1)}, bf16[512,256]{1,0:T(8,128)(2,1)S(1)}, u32[]{:S(2)}, u32[]{:S(2)}) collective-permute-start(bf16[512,256]{1,0:T(8,128)(2,1)S(1)} %select_convert_fusion), channel_id=1, source_target_pairs={{0,1},{1,0},{2,3},{3,2},{4,5},{5,4},{6,7},{7,6},{8,9},{9,8},{10,11... | collective-permute-start | bytes 786440 | tf_op jit(solution)/shard_map/ppermute | solution.py:138

commit v2 on v1

v2 whole, which is shorter than its diff:
```python
import jax
import jax.numpy as jnp
from jax import lax
from jax.experimental import pallas as pl
from jax.experimental.pallas import tpu as pltpu
from jax.sharding import PartitionSpec as P

KVH = 8
HD = 128
ROUNDS = 2
UNITS = 4
LOG2E = 1.4426950408889634
MASKED = -1e30
VMEM_LIMIT = 20 * 2**20


def dot(left, right, left_dim, right_dim):
    dims = (((left_dim,), (right_dim,)), ((), ()))
    return lax.dot_general(left, right, dims, preferred_element_type=jnp.float32)


def pack(place, *refs):
    ins, outs = refs[: 2 * UNITS], refs[2 * UNITS :]
    rows = ins[0].shape[0]
    for u, out in enumerate(outs):
        out[:rows, :] = ins[2 * u][...]
        out[rows:, :] = ins[2 * u + 1][...]


def finish(near0, near1, crossed, arrived0, arrived1, key_grad, value_grad):
    rows, width = key_grad.shape[0], near0.shape[1]
    for u, (near, arrived) in enumerate(((near0, arrived0), (near1, arrived1))):
        total = near[...] + crossed[u].astype(jnp.float32) + arrived[...].astype(jnp.float32)
        total = total.astype(jnp.bfloat16)
        key_grad[:, u * width : (u + 1) * width] = total[:rows]
        value_grad[:, u * width : (u + 1) * width] = total[rows:]


def attend(place, order, q0, q1, d0, d1, key, value, near_key, near_value, far1, far2, *outs):
    a0, a1, g0, g1, near, back1, back2 = outs
    rows = key.shape[0]
    scale = HD**-0.5
    position, size = place[0], order.shape[0]
    seen = [order[(position + size - r) % size] < order[position] for r in range(1, ROUNDS + 1)]
    first_core = position % 2 == 0
    key_row = lax.broadcasted_iota(jnp.int32, (rows, 2 * rows), 0)
    query_row = lax.broadcasted_iota(jnp.int32, (rows, 2 * rows), 1) % rows
    causal = key_row <= query_row
    for head in range(key.shape[1] // HD):
        c = slice(head * HD, (head + 1) * HD)
        query = jnp.concatenate([q0[:, c], q1[:, c]], 0)
        grad = jnp.concatenate([d0[:, c], d1[:, c]], 0)
        keys = [key[:, c], jnp.where(first_core, far1[:rows, c], near_key[:, c]), far2[:rows, c]]
        values = [value[:, c], jnp.where(first_core, far1[rows:, c], near_value[:, c]), far2[rows:, c]]
        scores = [dot(k, query, 1, 1) for k in keys]
        scores[0] = jnp.where(causal, scores[0], MASKED)
        top = jnp.max(scores[0], 0, keepdims=True)
        for s, visible in zip(scores[1:], seen):
            top = jnp.maximum(top, jnp.where(visible, jnp.max(s, 0, keepdims=True), MASKED))
        tops = [top] + [jnp.where(visible, top, -MASKED) for visible in seen]
        probs = [jnp.exp2((s - t) * (scale * LOG2E)) for s, t in zip(scores, tops)]
        inverse = 1.0 / sum(jnp.sum(p, 0, keepdims=True) for p in probs)
        probs = [p.astype(jnp.bfloat16) for p in probs]
        out = sum(dot(v, p, 0, 0) for v, p in zip(values, probs)) * inverse
        attended = out.T.astype(jnp.bfloat16)
        a0[:, c] = attended[:rows]
        a1[:, c] = attended[rows:]
        scaled = (grad.T.astype(jnp.float32) * inverse).astype(jnp.bfloat16)
        scaled_rows = scaled.T
        row_dot = jnp.sum(scaled.astype(jnp.float32) * out, 0, keepdims=True)
        query_grad = 0.0
        for k, v, p, ref in zip(keys, values, probs, (near, back1, back2)):
            ds = p * (dot(v, scaled, 1, 0) - row_dot).astype(jnp.bfloat16)
            ref[:rows, c] = (dot(ds, query, 1, 0) * scale).astype(ref.dtype)
            ref[rows:, c] = dot(p, scaled_rows, 1, 0).astype(ref.dtype)
            query_grad = query_grad + dot(k, ds, 0, 0)
        query_grad = (query_grad * scale).T.astype(jnp.bfloat16)
        g0[:, c] = query_grad[:rows]
        g1[:, c] = query_grad[rows:]


def unit_at(u, place):
    side = place[1]
    return jnp.where(u < UNITS // 2, 1 - side, side) * (UNITS // 2) + u % (UNITS // 2)


def pack_units(place, keys, values):
    rows, width = keys.shape[0], keys.shape[1] // UNITS
    specs = []
    for u in range(UNITS):
        specs += [pl.BlockSpec((rows, width), lambda t, place, u=u: (0, unit_at(u, place)))] * 2
    return pl.pallas_call(
        pack,
        grid_spec=pltpu.PrefetchScalarGridSpec(
            num_scalar_prefetch=1,
            grid=(1,),
            in_specs=specs,
            out_specs=[pl.BlockSpec((2 * rows, width), lambda t, place: (0, 0))] * UNITS,
        ),
        out_shape=[jax.ShapeDtypeStruct((2 * rows, width), keys.dtype)] * UNITS,
        compiler_params=pltpu.CompilerParams(vmem_limit_bytes=VMEM_LIMIT),
        cost_estimate=pl.CostEstimate(flops=0, bytes_accessed=8 * keys.size, transcendentals=0),
    )(place, *([keys, values] * UNITS))


def attend_unit(u, place, order, queries, out_grad, keys, values, near_keys, near_values, far1, far2):
    rows = keys.shape[0]
    width = far1.shape[1]
    heads = width // HD
    first = pl.BlockSpec((rows, width), lambda t, place, order: (0, unit_at(u, place)))
    second = pl.BlockSpec((rows, width), lambda t, place, order: (0, unit_at(u, place) + UNITS))
    single = pl.BlockSpec((rows, width), lambda t, place, order: (0, 0))
    double = pl.BlockSpec((2 * rows, width), lambda t, place, order: (0, 0))
    return pl.pallas_call(
        attend,
        grid_spec=pltpu.PrefetchScalarGridSpec(
            num_scalar_prefetch=2,
            grid=(1,),
            in_specs=[first, second, first, second, first, first, first, first, double, double],
            out_specs=[single] * 4 + [double] * 3,
        ),
        out_shape=[jax.ShapeDtypeStruct((rows, width), jnp.bfloat16)] * 4
        + [jax.ShapeDtypeStruct((2 * rows, width), jnp.float32)]
        + [jax.ShapeDtypeStruct((2 * rows, width), jnp.bfloat16)] * 2,
        compiler_params=pltpu.CompilerParams(vmem_limit_bytes=VMEM_LIMIT),
        cost_estimate=pl.CostEstimate(
            flops=6 * 2 * heads * (2 * rows) * (3 * rows) * HD,
            bytes_accessed=12 * rows * width * 2,
            transcendentals=heads * 6 * rows * rows,
        ),
    )(place, order, queries, queries, out_grad, out_grad, keys, values, near_keys, near_values, far1, far2)


def on_device(queries, keys, values, out_grad, block_position):
    size = lax.axis_size("cp")
    position = lax.axis_index("cp")
    core = position % 2
    side = lax.axis_index("kv")
    ahead = [(i, (i + 2) % size) for i in range(size)]
    behind = [((i + 2) % size, i) for i in range(size)]
    swap = [(i, i ^ 1) for i in range(size)]
    across = [(0, 1), (1, 0)]
    bf16, f32 = jnp.bfloat16, jnp.float32
    rows = keys.shape[0]
    zero = jnp.zeros((), f32)
    place = jnp.stack([position, side]).astype(jnp.int32)
    keys, values, queries, out_grad = [
        pltpu.with_memory_space_constraint(x, pltpu.HBM) for x in (keys, values, queries, out_grad)
    ]

    own = pack_units(place, keys, values)
    far2 = [lax.ppermute(x, "cp", ahead) for x in own]
    near_keys = lax.ppermute(keys, "cp", swap)
    near_values = lax.ppermute(values, "cp", swap)
    results, near, arrived = [], [], []
    crossed = []
    send = None
    for u in range(UNITS):
        if u:
            far2[u], _ = lax.optimization_barrier((far2[u], back1))
        far1 = lax.ppermute(far2[u], "cp", swap)
        if u:
            far1, _ = lax.optimization_barrier((far1, send))
        *outs, part, back1, back2 = attend_unit(
            u, place, block_position, queries, out_grad, keys, values, near_keys, near_values, far1, far2[u]
        )
        results.append(outs)
        got = lax.ppermute(back1, "cp", swap).astype(f32)
        near.append(part + jnp.where(core == 0, got, zero))
        send = back2.astype(f32) + jnp.where(core == 1, got, zero)
        if u < UNITS // 2:
            send = send.astype(bf16)
            crossed.append(lax.ppermute(send, "kv", across))
        else:
            send = (send + crossed[u - UNITS // 2].astype(f32)).astype(bf16)
            arrived.append(lax.ppermute(send, "cp", behind))
    near_crossed = lax.ppermute(jnp.stack([near[0], near[1]]).astype(bf16), "kv", across)
    key_grad, value_grad = pl.pallas_call(
        finish,
        out_shape=[jax.ShapeDtypeStruct((rows, keys.shape[1] // 2), bf16)] * 2,
        compiler_params=pltpu.CompilerParams(vmem_limit_bytes=VMEM_LIMIT),
    )(near[2], near[3], near_crossed, *arrived)

    def join(index):
        pieces = []
        for g in (0, 1):
            other = jnp.concatenate([results[0][index + g], results[1][index + g]], 1)
            mine = jnp.concatenate([results[2][index + g], results[3][index + g]], 1)
            pieces += [jnp.where(side == 0, mine, other), jnp.where(side == 0, other, mine)]
        return jnp.concatenate(pieces, 1)

    return join(0), join(2), key_grad, value_grad


def solution(mesh):
    placed = (P("cp", "kv"), P("cp", None), P("cp", None), P("cp", "kv"), P())
    return jax.shard_map(
        on_device,
        mesh=mesh,
        in_specs=placed,
        out_specs=(P("cp", "kv"), P("cp", "kv"), P("cp", "kv"), P("cp", "kv")),
        check_vma=False,
    )
```

time: 82.2 us -> 70.1 us (0.85)
  waiting for transfers between devices: 44.1 us -> 22.2 us
  starting transfers between devices: 10.8 us -> 17.9 us
  Pallas kernels: 18.7 us -> 24 us
  other arithmetic: 4.42 us -> 3.09 us
  local copies, waits for them, and re-layouts: 2.84 us -> 1.75 us
    ppermute x10 -> x19, waiting for transfers between devices: 44.1 us -> 22.2 us  [the longest x4 15.9 us: on_device(): far2 = [lax.ppermute(x, 'cp', ahead) for x in own]]
    ppermute x10 -> x19, starting transfers between devices: 10.8 us -> 17.9 us  [the longest x2 4.68 us: on_device(): crossed.append(lax.ppermute(send, 'kv', across))]
    pallas_call x2 -> x6, Pallas kernels: 18.7 us -> 24 us  [the longest x4 21.2 us: attend_unit(): pl.pallas_call(attend, grid_spec=pltpu.PrefetchScalarGridSpec(num_scalar_...]
    slice x3 -> x0, local copies, waits for them, and re-layouts: 1.41 us -> none  [the longest x1 1.37 us: columns(): x[:, chunk * half:(chunk + 1) * half]]
    select_n x3 -> x4, other arithmetic: 1.05 us -> 0.16 us  [join(): jnp.where(side == 0, mine, other)]
    unnamed x32 -> x14, local copies, waits for them, and re-layouts: 1.41 us -> 1.67 us
    concatenate x4 -> x2, other arithmetic: 2.31 us -> 2.19 us  [join(): return jnp.concatenate(pieces, 1)]
  transfers between devices with their start and end apart: 10 -> 19, of which waited for: 8 -> 7; matrix products, arithmetic and copies ran while one was open for 3% -> 5% of each run, Pallas kernels for 23% -> 30%
where the time goes in v2:
time: 70.1 us; the launch traced here: 69.9 us
  Pallas kernels  24 us (34%)
  waiting for transfers between devices  22.2 us (32%)
  starting transfers between devices  17.9 us (26%)
  other arithmetic  3.09 us (4%)
  local copies, waits for them, and re-layouts  1.75 us (2%)
  between operations  0.84 us (1%)
    pallas_call x4, Pallas kernels, attend_unit(): pl.pallas_call(attend, grid_spec=pltpu.PrefetchScalarGridSpec(num_scalar_...  21.2 us
    ppermute x4, waiting for transfers between devices, on_device(): far2 = [lax.ppermute(x, 'cp', ahead) for x in own]  15.9 us
    ppermute x2, starting transfers between devices, on_device(): crossed.append(lax.ppermute(send, 'kv', across))  4.68 us
    ppermute x2, waiting for transfers between devices, on_device(): arrived.append(lax.ppermute(send, 'cp', behind))  3.52 us
    ppermute x2, starting transfers between devices, on_device(): arrived.append(lax.ppermute(send, 'cp', behind))  3.24 us
    ppermute x4, starting transfers between devices, on_device(): far1 = lax.ppermute(far2[u], 'cp', swap)  2.85 us
    ppermute x4, starting transfers between devices, on_device(): far2 = [lax.ppermute(x, 'cp', ahead) for x in own]  2.55 us
    ppermute x4, starting transfers between devices, on_device(): got = lax.ppermute(back1, 'cp', swap).astype(f32)  2.24 us
  transfers between devices with their start and end apart: 19, of which 7 were waited for; matrix products, arithmetic and copies ran while one was open for 5% of the time, Pallas kernels for 30%

profile of v2, /device:TPU:1, one launch (start us, length us, event | category | flops | bytes accessed | tf_op | source)
XLA Modules:
  0.0 69.9 jit_solution(15444445557880369932)
XLA Ops:
  0.7 1.9 %shard_map.84 = (bf16[512,256]{1,0:T(8,128)(2,1)S(1)}, bf16[512,256]{1,0:T(8,128)(2,1)S(1)}, bf16[512,256]{1,0:T(8,128)(2,1)S(1)}, bf16[512,256]{1,0:T(8,128)(2,1)S(1)}) custom-call(s32[2]{0:T(128)S(1)} %pad_add_fusion.place, bf16[256,1024]{1,0:T(8,128)(2,1)} %key.7, bf16[256,1024]{1,0:T(8,128)(2,1)} %value.7, bf16[256,1024]{1,0:T(8,128)(2,1)} %key.7, ...), custom_call_target="tpu_custom_call" | custom-call | bytes 2097152 | tf_op jit(solution)/shard_map/pallas_call | solution.py:92
  2.6 2.5 %collective-permute-start.4 = (bf16[512,256]{1,0:T(8,128)(2,1)S(1)}, bf16[512,256]{1,0:T(8,128)(2,1)S(1)}, u32[]{:S(2)}, u32[]{:S(2)}) collective-permute-start(bf16[512,256]{1,0:T(8,128)(2,1)S(1)} %get-tuple-element.46), channel_id=1, source_target_pairs={{0,4},{2,6},{4,8},{6,10},{8,12},{10,14},{12,16},{14,18},{16,20},{1... | collective-permute-start | bytes 786440 | tf_op jit(solution)/shard_map/ppermute | solution.py:152
  5.2 1.0 %collective-permute-start = (bf16[256,1024]{1,0:T(8,128)(2,1)S(1)}, bf16[256,1024]{1,0:T(8,128)(2,1)S(1)}, u32[]{:S(2)}, u32[]{:S(2)}) collective-permute-start(bf16[256,1024]{1,0:T(8,128)(2,1)S(1)} %copy-done.1), channel_id=1, source_target_pairs={{0,2},{2,0},{4,6},{6,4},{8,10},{10,8},{12,14},{14,12},{16,18},{18,... | collective-permute-start | bytes 1572872 | tf_op jit(solution)/shard_map/ppermute | solution.py:153
  6.2 12.3 %collective-permute-done.4.far2 = bf16[512,256]{1,0:T(8,128)(2,1)S(1)} collective-permute-done((bf16[512,256]{1,0:T(8,128)(2,1)S(1)}, bf16[512,256]{1,0:T(8,128)(2,1)S(1)}, u32[]{:S(2)}, u32[]{:S(2)}) %collective-permute-start.4) | collective-permute-done | bytes 262176 | tf_op jit(solution)/shard_map/ppermute | solution.py:152
  18.5 1.2 %collective-permute-start.5 = (bf16[512,256]{1,0:T(8,128)(2,1)S(1)}, bf16[512,256]{1,0:T(8,128)(2,1)S(1)}, u32[]{:S(2)}, u32[]{:S(2)}) collective-permute-start(bf16[512,256]{1,0:T(8,128)(2,1)S(1)} %collective-permute-done.4.far2), channel_id=1, source_target_pairs={{0,2},{2,0},{4,6},{6,4},{8,10},{10,8},{12,14},{14,12},{16,18},{18,... | collective-permute-start | bytes 786440 | tf_op jit(solution)/shard_map/ppermute | solution.py:161
  19.8 1.2 %collective-permute-done.5.far1 = bf16[512,256]{1,0:T(8,128)(2,1)S(1)} collective-permute-done((bf16[512,256]{1,0:T(8,128)(2,1)S(1)}, bf16[512,256]{1,0:T(8,128)(2,1)S(1)}, u32[]{:S(2)}, u32[]{:S(2)}) %collective-permute-start.5) | collective-permute-done | bytes 262176 | tf_op jit(solution)/shard_map/ppermute | solution.py:161
  20.9 0.8 %copy-done.3 = bf16[256,1024]{1,0:T(8,128)(2,1)} copy-done((bf16[256,1024]{1,0:T(8,128)(2,1)}, bf16[256,1024]{1,0:T(8,128)(2,1)S(1)}, u32[]{:S(2)}) %copy-start.3) | copy-done | bytes 524312
  21.7 0.8 %copy-done.4 = bf16[256,1024]{1,0:T(8,128)(2,1)} copy-done((bf16[256,1024]{1,0:T(8,128)(2,1)}, bf16[256,1024]{1,0:T(8,128)(2,1)S(1)}, u32[]{:S(2)}) %copy-start.4) | copy-done | bytes 524312
  22.5 5.3 %shard_map.85 = (bf16[256,256]{1,0:T(8,128)(2,1)S(1)}, bf16[256,256]{1,0:T(8,128)(2,1)S(1)}, bf16[256,256]{1,0:T(8,128)(2,1)S(1)}, bf16[256,256]{1,0:T(8,128)(2,...) custom-call(s32[2]{0:T(128)S(1)} %pad_add_fusion.place, ...), custom_call_target="tpu_custom_call" | custom-call | flops 1207959552 | bytes 1572864 | tf_op jit(solution)/shard_map/pallas_call | solution.py:114
  27.8 0.5 collective-permute-start.7
  28.3 3.6 %collective-permute-done.3.far2 = bf16[512,256]{1,0:T(8,128)(2,1)S(1)} collective-permute-done((bf16[512,256]{1,0:T(8,128)(2,1)S(1)}, bf16[512,256]{1,0:T(8,128)(2,1)S(1)}, u32[]{:S(2)}, u32[]{:S(2)}) %collective-permute-start.3) | collective-permute-done | bytes 262176 | tf_op jit(solution)/shard_map/ppermute | solution.py:152
  31.9 0.8 %collective-permute-start.6 = (bf16[512,256]{1,0:T(8,128)(2,1)S(1)}, bf16[512,256]{1,0:T(8,128)(2,1)S(1)}, u32[]{:S(2)}, u32[]{:S(2)}) collective-permute-start(bf16[512,256]{1,0:T(8,128)(2,1)S(1)} %collective-permute-done.3.far2), channel_id=1, source_target_pairs={{0,2},{2,0},{4,6},{6,4},{8,10},{10,8},{12,14},{14,12},{16,18},{18,... | collective-permute-start | bytes 786440 | tf_op jit(solution)/shard_map/ppermute | solution.py:161
  32.9 2.7 %collective-permute-start.13 = (bf16[512,256]{1,0:T(8,128)(2,1)S(1)}, bf16[512,256]{1,0:T(8,128)(2,1)S(1)}, u32[]{:S(2)}, u32[]{:S(2)}) collective-permute-start(bf16[512,256]{1,0:T(8,128)(2,1)S(1)} %get-tuple-element.95), channel_id=1, source_target_pairs={{0,1},{1,0},{2,3},{3,2},{4,5},{5,4},{6,7},{7,6},{8,9},{9,8},{10,11... | collective-permute-start | bytes 786440 | tf_op jit(solution)/shard_map/ppermute | solution.py:173
  35.6 5.3 %shard_map.86 = (bf16[256,256]{1,0:T(8,128)(2,1)S(1)}, bf16[256,256]{1,0:T(8,128)(2,1)S(1)}, bf16[256,256]{1,0:T(8,128)(2,1)S(1)}, bf16[256,256]{1,0:T(8,128)(2,...) custom-call(s32[2]{0:T(128)S(1)} %pad_add_fusion.place, ...), custom_call_target="tpu_custom_call" | custom-call | flops 1207959552 | bytes 1572864 | tf_op jit(solution)/shard_map/pallas_call | solution.py:114
  40.9 0.4 collective-permute-start.9
  41.3 0.6 collective-permute-start.8
  42.0 0.6 collective-permute-done.9
  42.7 2.0 %collective-permute-start.17 = (bf16[512,256]{1,0:T(8,128)(2,1)S(1)}, bf16[512,256]{1,0:T(8,128)(2,1)S(1)}, u32[]{:S(2)}, u32[]{:S(2)}) collective-permute-start(bf16[512,256]{1,0:T(8,128)(2,1)S(1)} %get-tuple-element.97), channel_id=1, source_target_pairs={{0,1},{1,0},{2,3},{3,2},{4,5},{5,4},{6,7},{7,6},{8,9},{9,8},{10,11... | collective-permute-start | bytes 786440 | tf_op jit(solution)/shard_map/ppermute | solution.py:173
  44.7 5.3 %shard_map.87 = (bf16[256,256]{1,0:T(8,128)(2,1)S(1)}, bf16[256,256]{1,0:T(8,128)(2,1)S(1)}, bf16[256,256]{1,0:T(8,128)(2,1)S(1)}, bf16[256,256]{1,0:T(8,128)(2,...) custom-call(s32[2]{0:T(128)S(1)} %pad_add_fusion.place, ...), custom_call_target="tpu_custom_call" | custom-call | flops 1207959552 | bytes 1572864 | tf_op jit(solution)/shard_map/pallas_call | solution.py:114
  50.0 0.4 collective-permute-start.12
  50.3 0.2 collective-permute-start.11
  50.6 1.3 %collective-permute-start.15 = (bf16[2,512,256]{2,1,0:T(8,128)(2,1)S(1)}, bf16[2,512,256]{2,1,0:T(8,128)(2,1)S(1)}, u32[]{:S(2)}, u32[]{:S(2)}) collective-permute-start(bf16[2,512,256]{2,1,0:T(8,128)(2,1)S(1)} %pad_maximum_fusion.2), channel_id=1, source_target_pairs={{0,1},{1,0},{2,3},{3,2},{4,5},{5,4},{6,7},{7,6},{8,9},{9,8},{10,11... | collective-permute-start | bytes 1572872 | tf_op jit(solution)/shard_map/ppermute | solution.py:177
  52.2 1.5 %collective-permute-start.16 = (bf16[512,256]{1,0:T(8,128)(2,1)S(1)}, bf16[512,256]{1,0:T(8,128)(2,1)S(1)}, u32[]{:S(2)}, u32[]{:S(2)}) collective-permute-start(bf16[512,256]{1,0:T(8,128)(2,1)S(1)} %get-tuple-element.99), channel_id=1, source_target_pairs={{4,0},{6,2},{8,4},{10,6},{12,8},{14,10},{16,12},{18,14},{20,16},{2... | collective-permute-start | bytes 786440 | tf_op jit(solution)/shard_map/ppermute | solution.py:176
  53.7 5.3 %shard_map.88 = (bf16[256,256]{1,0:T(8,128)(2,1)S(1)}, bf16[256,256]{1,0:T(8,128)(2,1)S(1)}, bf16[256,256]{1,0:T(8,128)(2,1)S(1)}, bf16[256,256]{1,0:T(8,128)(2,...) custom-call(s32[2]{0:T(128)S(1)} %pad_add_fusion.place, ...), custom_call_target="tpu_custom_call" | custom-call | flops 1207959552 | bytes 1572864 | tf_op jit(solution)/shard_map/pallas_call | solution.py:114
  59.0 1.0 %collective-permute-start.14 = (bf16[512,256]{1,0:T(8,128)(2,1)S(1)}, bf16[512,256]{1,0:T(8,128)(2,1)S(1)}, u32[]{:S(2)}, u32[]{:S(2)}) collective-permute-start(bf16[512,256]{1,0:T(8,128)(2,1)S(1)} %get-tuple-element.78), channel_id=1, source_target_pairs={{0,2},{2,0},{4,6},{6,4},{8,10},{10,8},{12,14},{14,12},{16,18},{18,... | collective-permute-start | bytes 786440 | tf_op jit(solution)/shard_map/ppermute | solution.py:168
  60.3 0.9 %collective-permute-done.14 = bf16[512,256]{1,0:T(8,128)(2,1)S(1)} collective-permute-done((bf16[512,256]{1,0:T(8,128)(2,1)S(1)}, bf16[512,256]{1,0:T(8,128)(2,1)S(1)}, u32[]{:S(2)}, u32[]{:S(2)}) %collective-permute-start.14) | collective-permute-done | bytes 262176 | tf_op jit(solution)/shard_map/ppermute | solution.py:168
  61.2 0.2 fusion.15
  61.4 1.7 %collective-permute-start.18 = (bf16[512,256]{1,0:T(8,128)(2,1)S(1)}, bf16[512,256]{1,0:T(8,128)(2,1)S(1)}, u32[]{:S(2)}, u32[]{:S(2)}) collective-permute-start(bf16[512,256]{1,0:T(8,128)(2,1)S(1)} %get-tuple-element.92), channel_id=1, source_target_pairs={{4,0},{6,2},{8,4},{10,6},{12,8},{14,10},{16,12},{18,14},{20,16},{2... | collective-permute-start | bytes 786440 | tf_op jit(solution)/shard_map/ppermute | solution.py:176
  63.1 1.1 %pad_maximum_fusion.1 = bf16[256,2048]{1,0:T(8,128)(2,1)} fusion(bf16[256,512]{1,0:T(8,128)(2,1)S(1)} %get-tuple-element.87, bf16[256,512]{1,0:T(8,128)(2,1)S(1)} %get-tuple-element.86, bf16[256,512]{1,0:T(8,128)(2,1)S(1)} %get-tuple-element.85, bf16[256,512]{1,0:T(8,128)(2,1)S(1)} %get-tuple-element.84), kind=kLoop, calls=%fused_computation.1 | loop fusion | flops 4194304 | bytes 2097152 | tf_op jit(solution)/shard_map/concatenate | solution.py:190
  64.2 1.1 %pad_maximum_fusion = bf16[256,2048]{1,0:T(8,128)(2,1)} fusion(bf16[256,512]{1,0:T(8,128)(2,1)S(1)} %get-tuple-element.91, bf16[256,512]{1,0:T(8,128)(2,1)S(1)} %get-tuple-element.90, bf16[256,512]{1,0:T(8,128)(2,1)S(1)} %get-tuple-element.89, bf16[256,512]{1,0:T(8,128)(2,1)S(1)} %get-tuple-element.88), kind=kLoop, calls=%fused_computation | loop fusion | flops 4194304 | bytes 2097152 | tf_op jit(solution)/shard_map/concatenate | solution.py:190
  65.5 3.5 %collective-permute-done.18.arrived1 = bf16[512,256]{1,0:T(8,128)(2,1)S(1)} collective-permute-done((bf16[512,256]{1,0:T(8,128)(2,1)S(1)}, bf16[512,256]{1,0:T(8,128)(2,1)S(1)}, u32[]{:S(2)}, u32[]{:S(2)}) %collective-permute-start.18) | collective-permute-done | bytes 262176 | tf_op jit(solution)/shard_map/ppermute | solution.py:176
  69.0 0.9 %shard_map.89 = (bf16[256,512]{1,0:T(8,128)(2,1)}, bf16[256,512]{1,0:T(8,128)(2,1)}) custom-call(f32[512,256]{1,0:T(8,128)S(1)} %get-tuple-element.98.near0, f32[512,256]{1,0:T(8,128)S(1)} %get-tuple-element.93.near1, bf16[2,512,256]{2,1,0:T(8,128)(2,1)S(1)} %collective-permute-done.15.crossed, bf16[512,256]{1,0:T(8,128)(2,1)S(1)} %collective-permute-done.16.arrived0, ...), custom_call_target="tpu_custom_call" | custom-call | tf_op jit(solution)/shard_map/pallas_call | solution.py:178
  (46 shorter events, 1.2 us)
Async XLA Ops:
  0.7 4.5 %copy-start.1 = (bf16[256,1024]{1,0:T(8,128)(2,1)S(1)}, bf16[256,1024]{1,0:T(8,128)(2,1)}, u32[]{:S(2)}) copy-start(bf16[256,1024]{1,0:T(8,128)(2,1)} %key.7) | copy-start | bytes 1572868
  0.7 5.4 %copy-start.2 = (bf16[256,1024]{1,0:T(8,128)(2,1)S(1)}, bf16[256,1024]{1,0:T(8,128)(2,1)}, u32[]{:S(2)}) copy-start(bf16[256,1024]{1,0:T(8,128)(2,1)} %value.7) | copy-start | bytes 1572868
  0.7 21.8 %copy-start = (s32[128]{0:T(128)S(1)}, s32[128]{0:T(128)}, u32[]{:S(2)}) copy-start(s32[128]{0:T(128)} %order.7) | copy-start | bytes 1540
  2.6 15.9 %collective-permute-start.4 = (bf16[512,256]{1,0:T(8,128)(2,1)S(1)}, bf16[512,256]{1,0:T(8,128)(2,1)S(1)}, u32[]{:S(2)}, u32[]{:S(2)}) collective-permute-start(bf16[512,256]{1,0:T(8,128)(2,1)S(1)} %get-tuple-element.46), channel_id=1, source_target_pairs={{0,4},{2,6},{4,8},{6,10},{8,12},{10,14},{12,16},{14,18},{16,20},{1... | collective-permute-start | bytes 786440 | tf_op jit(solution)/shard_map/ppermute | solution.py:152
  5.2 15.7 %collective-permute-start = (bf16[256,1024]{1,0:T(8,128)(2,1)S(1)}, bf16[256,1024]{1,0:T(8,128)(2,1)S(1)}, u32[]{:S(2)}, u32[]{:S(2)}) collective-permute-start(bf16[256,1024]{1,0:T(8,128)(2,1)S(1)} %copy-done.1), channel_id=1, source_target_pairs={{0,2},{2,0},{4,6},{6,4},{8,10},{10,8},{12,14},{14,12},{16,18},{18,... | collective-permute-start | bytes 1572872 | tf_op jit(solution)/shard_map/ppermute | solution.py:153
  6.1 14.8 %collective-permute-start.1 = (bf16[256,1024]{1,0:T(8,128)(2,1)S(1)}, bf16[256,1024]{1,0:T(8,128)(2,1)S(1)}, u32[]{:S(2)}, u32[]{:S(2)}) collective-permute-start(bf16[256,1024]{1,0:T(8,128)(2,1)S(1)} %copy-done.2), channel_id=1, source_target_pairs={{0,2},{2,0},{4,6},{6,4},{8,10},{10,8},{12,14},{14,12},{16,18},{18,... | collective-permute-start | bytes 1572872 | tf_op jit(solution)/shard_map/ppermute | solution.py:154
  18.5 2.4 %collective-permute-start.5 = (bf16[512,256]{1,0:T(8,128)(2,1)S(1)}, bf16[512,256]{1,0:T(8,128)(2,1)S(1)}, u32[]{:S(2)}, u32[]{:S(2)}) collective-permute-start(bf16[512,256]{1,0:T(8,128)(2,1)S(1)} %collective-permute-done.4.far2), channel_id=1, source_target_pairs={{0,2},{2,0},{4,6},{6,4},{8,10},{10,8},{12,14},{14,12},{16,18},{18,... | collective-permute-start | bytes 786440 | tf_op jit(solution)/shard_map/ppermute | solution.py:161
  19.8 12.2 %collective-permute-start.3 = (bf16[512,256]{1,0:T(8,128)(2,1)S(1)}, bf16[512,256]{1,0:T(8,128)(2,1)S(1)}, u32[]{:S(2)}, u32[]{:S(2)}) collective-permute-start(bf16[512,256]{1,0:T(8,128)(2,1)S(1)} %get-tuple-element.45), channel_id=1, source_target_pairs={{0,4},{2,6},{4,8},{6,10},{8,12},{10,14},{12,16},{14,18},{16,20},{1... | collective-permute-start | bytes 786440 | tf_op jit(solution)/shard_map/ppermute | solution.py:152
  20.9 0.8 %copy-start.3 = (bf16[256,1024]{1,0:T(8,128)(2,1)}, bf16[256,1024]{1,0:T(8,128)(2,1)S(1)}, u32[]{:S(2)}) copy-start(bf16[256,1024]{1,0:T(8,128)(2,1)S(1)} %collective-permute-done.near_key) | copy-start | bytes 1572868
  21.7 0.8 %copy-start.4 = (bf16[256,1024]{1,0:T(8,128)(2,1)}, bf16[256,1024]{1,0:T(8,128)(2,1)S(1)}, u32[]{:S(2)}) copy-start(bf16[256,1024]{1,0:T(8,128)(2,1)S(1)} %collective-permute-done.1.near_value) | copy-start | bytes 1572868
  27.8 4.9 %collective-permute-start.7 = (bf16[512,256]{1,0:T(8,128)(2,1)S(1)}, bf16[512,256]{1,0:T(8,128)(2,1)S(1)}, u32[]{:S(2)}, u32[]{:S(2)}) collective-permute-start(bf16[512,256]{1,0:T(8,128)(2,1)S(1)} %get-tuple-element.47), channel_id=1, source_target_pairs={{0,2},{2,0},{4,6},{6,4},{8,10},{10,8},{12,14},{14,12},{16,18},{18,... | collective-permute-start | bytes 786440 | tf_op jit(solution)/shard_map/ppermute | solution.py:168
  28.3 13.0 %collective-permute-start.2 = (bf16[512,256]{1,0:T(8,128)(2,1)S(1)}, bf16[512,256]{1,0:T(8,128)(2,1)S(1)}, u32[]{:S(2)}, u32[]{:S(2)}) collective-permute-start(bf16[512,256]{1,0:T(8,128)(2,1)S(1)} %get-tuple-element.44), channel_id=1, source_target_pairs={{0,4},{2,6},{4,8},{6,10},{8,12},{10,14},{12,16},{14,18},{16,20},{1... | collective-permute-start | bytes 786440 | tf_op jit(solution)/shard_map/ppermute | solution.py:152
  28.3 22.0 %collective-permute-start.10 = (bf16[512,256]{1,0:T(8,128)(2,1)S(1)}, bf16[512,256]{1,0:T(8,128)(2,1)S(1)}, u32[]{:S(2)}, u32[]{:S(2)}) collective-permute-start(bf16[512,256]{1,0:T(8,128)(2,1)S(1)} %get-tuple-element.56), channel_id=1, source_target_pairs={{0,4},{2,6},{4,8},{6,10},{8,12},{10,14},{12,16},{14,18},{16,20},{1... | collective-permute-start | bytes 786440 | tf_op jit(solution)/shard_map/ppermute | solution.py:152
  31.9 3.7 %collective-permute-start.6 = (bf16[512,256]{1,0:T(8,128)(2,1)S(1)}, bf16[512,256]{1,0:T(8,128)(2,1)S(1)}, u32[]{:S(2)}, u32[]{:S(2)}) collective-permute-start(bf16[512,256]{1,0:T(8,128)(2,1)S(1)} %collective-permute-done.3.far2), channel_id=1, source_target_pairs={{0,2},{2,0},{4,6},{6,4},{8,10},{10,8},{12,14},{14,12},{16,18},{18,... | collective-permute-start | bytes 786440 | tf_op jit(solution)/shard_map/ppermute | solution.py:161
  32.9 19.1 %collective-permute-start.13 = (bf16[512,256]{1,0:T(8,128)(2,1)S(1)}, bf16[512,256]{1,0:T(8,128)(2,1)S(1)}, u32[]{:S(2)}, u32[]{:S(2)}) collective-permute-start(bf16[512,256]{1,0:T(8,128)(2,1)S(1)} %get-tuple-element.95), channel_id=1, source_target_pairs={{0,1},{1,0},{2,3},{3,2},{4,5},{5,4},{6,7},{7,6},{8,9},{9,8},{10,11... | collective-permute-start | bytes 786440 | tf_op jit(solution)/shard_map/ppermute | solution.py:173
  40.9 1.6 %collective-permute-start.9 = (bf16[512,256]{1,0:T(8,128)(2,1)S(1)}, bf16[512,256]{1,0:T(8,128)(2,1)S(1)}, u32[]{:S(2)}, u32[]{:S(2)}) collective-permute-start(bf16[512,256]{1,0:T(8,128)(2,1)S(1)} %get-tuple-element.51), channel_id=1, source_target_pairs={{0,2},{2,0},{4,6},{6,4},{8,10},{10,8},{12,14},{14,12},{16,18},{18,... | collective-permute-start | bytes 786440 | tf_op jit(solution)/shard_map/ppermute | solution.py:168
  41.3 3.4 %collective-permute-start.8 = (bf16[512,256]{1,0:T(8,128)(2,1)S(1)}, bf16[512,256]{1,0:T(8,128)(2,1)S(1)}, u32[]{:S(2)}, u32[]{:S(2)}) collective-permute-start(bf16[512,256]{1,0:T(8,128)(2,1)S(1)} %collective-permute-done.2.far2), channel_id=1, source_target_pairs={{0,2},{2,0},{4,6},{6,4},{8,10},{10,8},{12,14},{14,12},{16,18},{18,... | collective-permute-start | bytes 786440 | tf_op jit(solution)/shard_map/ppermute | solution.py:161
  42.7 17.6 %collective-permute-start.17 = (bf16[512,256]{1,0:T(8,128)(2,1)S(1)}, bf16[512,256]{1,0:T(8,128)(2,1)S(1)}, u32[]{:S(2)}, u32[]{:S(2)}) collective-permute-start(bf16[512,256]{1,0:T(8,128)(2,1)S(1)} %get-tuple-element.97), channel_id=1, source_target_pairs={{0,1},{1,0},{2,3},{3,2},{4,5},{5,4},{6,7},{7,6},{8,9},{9,8},{10,11... | collective-permute-start | bytes 786440 | tf_op jit(solution)/shard_map/ppermute | solution.py:173
  50.0 2.1 %collective-permute-start.12 = (bf16[512,256]{1,0:T(8,128)(2,1)S(1)}, bf16[512,256]{1,0:T(8,128)(2,1)S(1)}, u32[]{:S(2)}, u32[]{:S(2)}) collective-permute-start(bf16[512,256]{1,0:T(8,128)(2,1)S(1)} %get-tuple-element.57), channel_id=1, source_target_pairs={{0,2},{2,0},{4,6},{6,4},{8,10},{10,8},{12,14},{14,12},{16,18},{18,... | collective-permute-start | bytes 786440 | tf_op jit(solution)/shard_map/ppermute | solution.py:168
  50.3 3.4 %collective-permute-start.11 = (bf16[512,256]{1,0:T(8,128)(2,1)S(1)}, bf16[512,256]{1,0:T(8,128)(2,1)S(1)}, u32[]{:S(2)}, u32[]{:S(2)}) collective-permute-start(bf16[512,256]{1,0:T(8,128)(2,1)S(1)} %collective-permute-done.10.far2), channel_id=1, source_target_pairs={{0,2},{2,0},{4,6},{6,4},{8,10},{10,8},{12,14},{14,12},{16,18},{18,... | collective-permute-start | bytes 786440 | tf_op jit(solution)/shard_map/ppermute | solution.py:161
  50.6 14.8 %collective-permute-start.15 = (bf16[2,512,256]{2,1,0:T(8,128)(2,1)S(1)}, bf16[2,512,256]{2,1,0:T(8,128)(2,1)S(1)}, u32[]{:S(2)}, u32[]{:S(2)}) collective-permute-start(bf16[2,512,256]{2,1,0:T(8,128)(2,1)S(1)} %pad_maximum_fusion.2), channel_id=1, source_target_pairs={{0,1},{1,0},{2,3},{3,2},{4,5},{5,4},{6,7},{7,6},{8,9},{9,8},{10,11... | collective-permute-start | bytes 1572872 | tf_op jit(solution)/shard_map/ppermute | solution.py:177
  52.2 13.3 %collective-permute-start.16 = (bf16[512,256]{1,0:T(8,128)(2,1)S(1)}, bf16[512,256]{1,0:T(8,128)(2,1)S(1)}, u32[]{:S(2)}, u32[]{:S(2)}) collective-permute-start(bf16[512,256]{1,0:T(8,128)(2,1)S(1)} %get-tuple-element.99), channel_id=1, source_target_pairs={{4,0},{6,2},{8,4},{10,6},{12,8},{14,10},{16,12},{18,14},{20,16},{2... | collective-permute-start | bytes 786440 | tf_op jit(solution)/shard_map/ppermute | solution.py:176
  59.0 2.2 %collective-permute-start.14 = (bf16[512,256]{1,0:T(8,128)(2,1)S(1)}, bf16[512,256]{1,0:T(8,128)(2,1)S(1)}, u32[]{:S(2)}, u32[]{:S(2)}) collective-permute-start(bf16[512,256]{1,0:T(8,128)(2,1)S(1)} %get-tuple-element.78), channel_id=1, source_target_pairs={{0,2},{2,0},{4,6},{6,4},{8,10},{10,8},{12,14},{14,12},{16,18},{18,... | collective-permute-start | bytes 786440 | tf_op jit(solution)/shard_map/ppermute | solution.py:168
  61.4 7.6 %collective-permute-start.18 = (bf16[512,256]{1,0:T(8,128)(2,1)S(1)}, bf16[512,256]{1,0:T(8,128)(2,1)S(1)}, u32[]{:S(2)}, u32[]{:S(2)}) collective-permute-start(bf16[512,256]{1,0:T(8,128)(2,1)S(1)} %get-tuple-element.92), channel_id=1, source_target_pairs={{4,0},{6,2},{8,4},{10,6},{12,8},{14,10},{16,12},{18,14},{20,16},{2... | collective-permute-start | bytes 786440 | tf_op jit(solution)/shard_map/ppermute | solution.py:176

commit v3 on v2

--- a/solution.py
+++ b/solution.py
@@ -27,6 +27,15 @@
         out[rows:, :] = ins[2 * u + 1][...]
 
 
+def stage(place, *refs):
+    ins, outs = refs[: 8 * UNITS], refs[8 * UNITS :]
+    rows, width = ins[0].shape
+    for u, out in enumerate(outs):
+        for n in range(8):
+            at = slice(n // 2 * width, (n // 2 + 1) * width)
+            out[n % 2 * rows : (n % 2 + 1) * rows, at] = ins[8 * u + n][...]
+
+
 def finish(near0, near1, crossed, arrived0, arrived1, key_grad, value_grad):
     rows, width = key_grad.shape[0], near0.shape[1]
     for u, (near, arrived) in enumerate(((near0, arrived0), (near1, arrived1))):
@@ -36,9 +45,9 @@
         value_grad[:, u * width : (u + 1) * width] = total[rows:]
 
 
-def attend(place, order, q0, q1, d0, d1, key, value, near_key, near_value, far1, far2, *outs):
+def attend(place, order, heads, far1, far2, *outs):
     a0, a1, g0, g1, near, back1, back2 = outs
-    rows = key.shape[0]
+    rows, width = far1.shape[0] // 2, far1.shape[1]
     scale = HD**-0.5
     position, size = place[0], order.shape[0]
     seen = [order[(position + size - r) % size] < order[position] for r in range(1, ROUNDS + 1)]
@@ -46,12 +55,11 @@
     key_row = lax.broadcasted_iota(jnp.int32, (rows, 2 * rows), 0)
     query_row = lax.broadcasted_iota(jnp.int32, (rows, 2 * rows), 1) % rows
     causal = key_row <= query_row
-    for head in range(key.shape[1] // HD):
+    for head in range(width // HD):
         c = slice(head * HD, (head + 1) * HD)
-        query = jnp.concatenate([q0[:, c], q1[:, c]], 0)
-        grad = jnp.concatenate([d0[:, c], d1[:, c]], 0)
-        keys = [key[:, c], jnp.where(first_core, far1[:rows, c], near_key[:, c]), far2[:rows, c]]
-        values = [value[:, c], jnp.where(first_core, far1[rows:, c], near_value[:, c]), far2[rows:, c]]
+        query, grad, own, beside = [heads[:, n * width + head * HD : n * width + (head + 1) * HD] for n in range(4)]
+        keys = [own[:rows], jnp.where(first_core, far1[:rows, c], beside[:rows]), far2[:rows, c]]
+        values = [own[rows:], jnp.where(first_core, far1[rows:, c], beside[rows:]), far2[rows:, c]]
         scores = [dot(k, query, 1, 1) for k in keys]
         scores[0] = jnp.where(causal, scores[0], MASKED)
         top = jnp.max(scores[0], 0, keepdims=True)
@@ -103,12 +111,31 @@
     )(place, *([keys, values] * UNITS))
 
 
-def attend_unit(u, place, order, queries, out_grad, keys, values, near_keys, near_values, far1, far2):
-    rows = keys.shape[0]
+def stage_heads(place, queries, out_grad, keys, values, near_keys, near_values, width):
+    rows = queries.shape[0]
+    specs = [
+        pl.BlockSpec((rows, width), lambda t, place, u=u, g=g: (0, unit_at(u, place) + g * UNITS))
+        for u in range(UNITS)
+        for g in (0, 1, 0, 1, 0, 0, 0, 0)
+    ]
+    shape = (2 * rows, 4 * width)
+    return pl.pallas_call(
+        stage,
+        grid_spec=pltpu.PrefetchScalarGridSpec(
+            num_scalar_prefetch=1,
+            grid=(1,),
+            in_specs=specs,
+            out_specs=[pl.BlockSpec(shape, lambda t, place: (0, 0))] * UNITS,
+        ),
+        out_shape=[jax.ShapeDtypeStruct(shape, queries.dtype)] + [pltpu.HBM(shape, queries.dtype)] * (UNITS - 1),
+        compiler_params=pltpu.CompilerParams(vmem_limit_bytes=VMEM_LIMIT),
+    )(place, *([queries, queries, out_grad, out_grad, keys, values, near_keys, near_values] * UNITS))
+
+
+def attend_unit(u, place, order, heads, far1, far2):
+    rows = far1.shape[0] // 2
     width = far1.shape[1]
-    heads = width // HD
-    first = pl.BlockSpec((rows, width), lambda t, place, order: (0, unit_at(u, place)))
-    second = pl.BlockSpec((rows, width), lambda t, place, order: (0, unit_at(u, place) + UNITS))
+    staged = pl.BlockSpec((2 * rows, 4 * width), lambda t, place, order: (0, 0))
     single = pl.BlockSpec((rows, width), lambda t, place, order: (0, 0))
     double = pl.BlockSpec((2 * rows, width), lambda t, place, order: (0, 0))
     return pl.pallas_call(
@@ -116,19 +143,13 @@
         grid_spec=pltpu.PrefetchScalarGridSpec(
             num_scalar_prefetch=2,
             grid=(1,),
-            in_specs=[first, second, first, second, first, first, first, first, double, double],
+            in_specs=[staged, double, double],
             out_specs=[single] * 4 + [double] * 3,
         ),
         out_shape=[jax.ShapeDtypeStruct((rows, width), jnp.bfloat16)] * 4
-        + [jax.ShapeDtypeStruct((2 * rows, width), jnp.float32)]
-        + [jax.ShapeDtypeStruct((2 * rows, width), jnp.bfloat16)] * 2,
-        compiler_params=pltpu.CompilerParams(vmem_limit_bytes=VMEM_LIMIT),
-        cost_estimate=pl.CostEstimate(
-            flops=6 * 2 * heads * (2 * rows) * (3 * rows) * HD,
-            bytes_accessed=12 * rows * width * 2,
-            transcendentals=heads * 6 * rows * rows,
-        ),
-    )(place, order, queries, queries, out_grad, out_grad, keys, values, near_keys, near_values, far1, far2)
+        + [jax.ShapeDtypeStruct((2 * rows, width), jnp.bfloat16)] * 3,
+        compiler_params=pltpu.CompilerParams(vmem_limit_bytes=VMEM_LIMIT),
+    )(place, order, heads, far1, far2)
 
 
 def on_device(queries, keys, values, out_grad, block_position):
@@ -144,14 +165,20 @@
     rows = keys.shape[0]
     zero = jnp.zeros((), f32)
     place = jnp.stack([position, side]).astype(jnp.int32)
+    raw_keys, raw_values = keys, values
     keys, values, queries, out_grad = [
         pltpu.with_memory_space_constraint(x, pltpu.HBM) for x in (keys, values, queries, out_grad)
     ]
 
     own = pack_units(place, keys, values)
     far2 = [lax.ppermute(x, "cp", ahead) for x in own]
-    near_keys = lax.ppermute(keys, "cp", swap)
-    near_values = lax.ppermute(values, "cp", swap)
+    raw_keys, raw_values, _ = lax.optimization_barrier((raw_keys, raw_values, own[0]))
+    near_keys = lax.ppermute(raw_keys, "cp", swap)
+    near_values = lax.ppermute(raw_values, "cp", swap)
+    heads = stage_heads(
+        place, queries, out_grad, keys, values, near_keys, near_values, own[0].shape[1]
+    )
+    far2[0], _ = lax.optimization_barrier((far2[0], heads[0]))
     results, near, arrived = [], [], []
     crossed = []
     send = None
@@ -162,7 +189,7 @@
         if u:
             far1, _ = lax.optimization_barrier((far1, send))
         *outs, part, back1, back2 = attend_unit(
-            u, place, block_position, queries, out_grad, keys, values, near_keys, near_values, far1, far2[u]
+            u, place, block_position, heads[u], far1, far2[u]
         )
         results.append(outs)
         got = lax.ppermute(back1, "cp", swap).astype(f32)

time: 70.1 us -> 66.4 us (0.947)
  starting transfers between devices: 17.9 us -> 14 us
  waiting for transfers between devices: 22.2 us -> 23.9 us
  local copies, waits for them, and re-layouts: 1.75 us -> 0.88 us
    pallas_call x4, Pallas kernels: 21.2 us -> 16.1 us  [attend_unit(): pl.pallas_call(attend, grid_spec=pltpu.PrefetchScalarGridSpec(num_scalar_...]
    pallas_call x0 -> x1, Pallas kernels: none -> 4.46 us  [stage_heads(): pl.pallas_call(stage, grid_spec=pltpu.PrefetchScalarGridSpec(num_scalar_p...]
    ppermute x1, waiting for transfers between devices: 0.14 us -> 3.3 us  [on_device(): lax.ppermute(jnp.stack([near[0], near[1]]).astype(bf16), 'kv', across)]
    ppermute x2, starting transfers between devices: 3.24 us -> 0.39 us  [on_device(): arrived.append(lax.ppermute(send, 'cp', behind))]
    ppermute x4, starting transfers between devices: 2.55 us -> 0.01 us  [on_device(): far2 = [lax.ppermute(x, 'cp', ahead) for x in own]]
    ppermute x4, waiting for transfers between devices: 15.9 us -> 13.4 us  [on_device(): far2 = [lax.ppermute(x, 'cp', ahead) for x in own]]
    ppermute x2, starting transfers between devices: 1.05 us -> 3.43 us  [the longest x1 3.33 us: on_device(): near_keys = lax.ppermute(raw_keys, 'cp', swap)]
    ppermute x2, waiting for transfers between devices: 0.01 us -> 2.17 us  [the longest x1 1.42 us: on_device(): near_keys = lax.ppermute(raw_keys, 'cp', swap)]
  transfers between devices with their start and end apart: 19 -> 19, of which waited for: 7 -> 9; matrix products, arithmetic and copies ran while one was open for 5% -> 5% of each run, Pallas kernels for 30% -> 31%
where the time goes in v3:
time: 66.4 us; the launch traced here: 66.2 us
  waiting for transfers between devices  23.9 us (36%)
  Pallas kernels  23.4 us (35%)
  starting transfers between devices  14 us (21%)
  other arithmetic  3.14 us (5%)
  between operations  0.9 us (1%)
  local copies, waits for them, and re-layouts  0.88 us (1%)
    pallas_call x4, Pallas kernels, attend_unit(): pl.pallas_call(attend, grid_spec=pltpu.PrefetchScalarGridSpec(num_scalar_...  16.1 us
    ppermute x4, waiting for transfers between devices, on_device(): far2 = [lax.ppermute(x, 'cp', ahead) for x in own]  13.4 us
    pallas_call x1, Pallas kernels, stage_heads(): pl.pallas_call(stage, grid_spec=pltpu.PrefetchScalarGridSpec(num_scalar_p...  4.46 us
    ppermute x2, starting transfers between devices, on_device(): crossed.append(lax.ppermute(send, 'kv', across))  3.55 us
    ppermute x1, starting transfers between devices, on_device(): near_keys = lax.ppermute(raw_keys, 'cp', swap)  3.33 us
    ppermute x1, waiting for transfers between devices, on_device(): lax.ppermute(jnp.stack([near[0], near[1]]).astype(bf16), 'kv', across)  3.3 us
    ppermute x1, starting transfers between devices, on_device(): lax.ppermute(jnp.stack([near[0], near[1]]).astype(bf16), 'kv', across)  2.28 us
    ppermute x4, starting transfers between devices, on_device(): got = lax.ppermute(back1, 'cp', swap).astype(f32)  2.27 us
  transfers between devices with their start and end apart: 19, of which 9 were waited for; matrix products, arithmetic and copies ran while one was open for 5% of the time, Pallas kernels for 31%

profile of v3, /device:TPU:1, one launch (start us, length us, event | category | flops | bytes accessed | tf_op | source)
XLA Modules:
  0.0 66.2 jit_solution(5286681951797402848)
XLA Ops:
  0.7 1.9 %shard_map.84 = (bf16[512,256]{1,0:T(8,128)(2,1)S(1)}, bf16[512,256]{1,0:T(8,128)(2,1)S(1)}, bf16[512,256]{1,0:T(8,128)(2,1)S(1)}, bf16[512,256]{1,0:T(8,128)(2,1)S(1)}) custom-call(s32[2]{0:T(128)S(1)} %pad_add_fusion.place, bf16[256,1024]{1,0:T(8,128)(2,1)} %refs_28_.1, bf16[256,1024]{1,0:T(8,128)(2,1)} %refs_29_.1, bf16[256,1024]{1,0:T(8,128)(2,1)} %refs_28_.1, ...), custom_call_target="tpu_custom_call" | custom-call | bytes 2097152 | tf_op jit(solution)/shard_map/pallas_call | solution.py:100
  2.6 3.3 %collective-permute-start = (bf16[256,1024]{1,0:T(8,128)(2,1)S(1)}, bf16[256,1024]{1,0:T(8,128)(2,1)S(1)}, u32[]{:S(2)}, u32[]{:S(2)}) collective-permute-start(bf16[256,1024]{1,0:T(8,128)(2,1)S(1)} %copy-done.4), channel_id=1, source_target_pairs={{0,2},{2,0},{4,6},{6,4},{8,10},{10,8},{12,14},{14,12},{16,18},{18,... | collective-permute-start | bytes 1572872 | tf_op jit(solution)/shard_map/ppermute | solution.py:176
  6.1 1.4 %collective-permute-done.refs_6_.refs_14_.refs_22_.refs_30_ = bf16[256,1024]{1,0:T(8,128)(2,1)S(1)} collective-permute-done((bf16[256,1024]{1,0:T(8,128)(2,1)S(1)}, bf16[256,1024]{1,0:T(8,128)(2,1)S(1)}, u32[]{:S(2)}, u32[]{:S(2)}) %collective-permute-start) | collective-permute-done | bytes 524320 | tf_op jit(solution)/shard_map/ppermute | solution.py:176
  7.5 0.7 %collective-permute-done.1.refs_7_.refs_15_.refs_23_.refs_31_ = bf16[256,1024]{1,0:T(8,128)(2,1)S(1)} collective-permute-done((bf16[256,1024]{1,0:T(8,128)(2,1)S(1)}, bf16[256,1024]{1,0:T(8,128)(2,1)S(1)}, u32[]{:S(2)}, u32[]{:S(2)}) %collective-permute-start.1) | collective-permute-done | bytes 524320 | tf_op jit(solution)/shard_map/ppermute | solution.py:177
  8.3 4.5 %shard_map.85 = (bf16[512,1024]{1,0:T(8,128)(2,1)S(1)}, bf16[512,1024]{1,0:T(8,128)(2,1)}, bf16[512,1024]{1,0:T(8,128)(2,1)}, bf16[512,1024]{1,0:T(8,128)(2,1)}) custom-call(s32[2]{0:T(128)S(1)} %pad_add_fusion.place, bf16[256,2048]{1,0:T(8,128)(2,1)} %refs_25_.1, bf16[256,2048]{1,0:T(8,128)(2,1)} %refs_25_.1, bf16[256,2048]{1,0:T(8,128)(2,1)} %refs_27_.1, ...), custom_call_target="tpu_custom_call" | custom-call | tf_op jit(solution)/shard_map/pallas_call | solution.py:122
  12.7 6.9 %collective-permute-done.4.far2 = bf16[512,256]{1,0:T(8,128)(2,1)S(1)} collective-permute-done((bf16[512,256]{1,0:T(8,128)(2,1)S(1)}, bf16[512,256]{1,0:T(8,128)(2,1)S(1)}, u32[]{:S(2)}, u32[]{:S(2)}) %collective-permute-start.4) | collective-permute-done | bytes 262176 | tf_op jit(solution)/shard_map/ppermute | solution.py:174
  19.6 0.9 %collective-permute-start.5 = (bf16[512,256]{1,0:T(8,128)(2,1)S(1)}, bf16[512,256]{1,0:T(8,128)(2,1)S(1)}, u32[]{:S(2)}, u32[]{:S(2)}) collective-permute-start(bf16[512,256]{1,0:T(8,128)(2,1)S(1)} %collective-permute-done.4.far2), channel_id=1, source_target_pairs={{0,2},{2,0},{4,6},{6,4},{8,10},{10,8},{12,14},{14,12},{16,18},{18,... | collective-permute-start | bytes 786440 | tf_op jit(solution)/shard_map/ppermute | solution.py:188
  20.6 1.2 %collective-permute-done.5.far1 = bf16[512,256]{1,0:T(8,128)(2,1)S(1)} collective-permute-done((bf16[512,256]{1,0:T(8,128)(2,1)S(1)}, bf16[512,256]{1,0:T(8,128)(2,1)S(1)}, u32[]{:S(2)}, u32[]{:S(2)}) %collective-permute-start.5) | collective-permute-done | bytes 262176 | tf_op jit(solution)/shard_map/ppermute | solution.py:188
  21.7 4.0 %shard_map.86 = (bf16[256,256]{1,0:T(8,128)(2,1)S(1)}, bf16[256,256]{1,0:T(8,128)(2,1)S(1)}, bf16[256,256]{1,0:T(8,128)(2,1)S(1)}, bf16[256,256]{1,0:T(8,128)(2,...) custom-call(s32[2]{0:T(128)S(1)} %pad_add_fusion.place, ...), custom_call_target="tpu_custom_call" | custom-call | tf_op jit(solution)/shard_map/pallas_call | solution.py:141
  25.8 0.5 collective-permute-start.7
  26.2 6.5 %collective-permute-done.3.far2 = bf16[512,256]{1,0:T(8,128)(2,1)S(1)} collective-permute-done((bf16[512,256]{1,0:T(8,128)(2,1)S(1)}, bf16[512,256]{1,0:T(8,128)(2,1)S(1)}, u32[]{:S(2)}, u32[]{:S(2)}) %collective-permute-start.3) | collective-permute-done | bytes 262176 | tf_op jit(solution)/shard_map/ppermute | solution.py:174
  32.7 0.8 %collective-permute-start.6 = (bf16[512,256]{1,0:T(8,128)(2,1)S(1)}, bf16[512,256]{1,0:T(8,128)(2,1)S(1)}, u32[]{:S(2)}, u32[]{:S(2)}) collective-permute-start(bf16[512,256]{1,0:T(8,128)(2,1)S(1)} %collective-permute-done.3.far2), channel_id=1, source_target_pairs={{0,2},{2,0},{4,6},{6,4},{8,10},{10,8},{12,14},{14,12},{16,18},{18,... | collective-permute-start | bytes 786440 | tf_op jit(solution)/shard_map/ppermute | solution.py:188
  33.7 2.7 %collective-permute-start.13 = (bf16[512,256]{1,0:T(8,128)(2,1)S(1)}, bf16[512,256]{1,0:T(8,128)(2,1)S(1)}, u32[]{:S(2)}, u32[]{:S(2)}) collective-permute-start(bf16[512,256]{1,0:T(8,128)(2,1)S(1)} %get-tuple-element.109), channel_id=1, source_target_pairs={{0,1},{1,0},{2,3},{3,2},{4,5},{5,4},{6,7},{7,6},{8,9},{9,8},{10,11... | collective-permute-start | bytes 786440 | tf_op jit(solution)/shard_map/ppermute | solution.py:200
  36.5 4.0 %shard_map.87 = (bf16[256,256]{1,0:T(8,128)(2,1)S(1)}, bf16[256,256]{1,0:T(8,128)(2,1)S(1)}, bf16[256,256]{1,0:T(8,128)(2,1)S(1)}, bf16[256,256]{1,0:T(8,128)(2,...) custom-call(s32[2]{0:T(128)S(1)} %pad_add_fusion.place, ...), custom_call_target="tpu_custom_call" | custom-call | tf_op jit(solution)/shard_map/pallas_call | solution.py:141
  40.5 0.4 collective-permute-start.9
  40.9 0.2 collective-permute-start.8
  41.2 0.9 %collective-permute-done.9 = bf16[512,256]{1,0:T(8,128)(2,1)S(1)} collective-permute-done((bf16[512,256]{1,0:T(8,128)(2,1)S(1)}, bf16[512,256]{1,0:T(8,128)(2,1)S(1)}, u32[]{:S(2)}, u32[]{:S(2)}) %collective-permute-start.9) | collective-permute-done | bytes 262176 | tf_op jit(solution)/shard_map/ppermute | solution.py:195
  42.3 0.8 %collective-permute-start.17 = (bf16[512,256]{1,0:T(8,128)(2,1)S(1)}, bf16[512,256]{1,0:T(8,128)(2,1)S(1)}, u32[]{:S(2)}, u32[]{:S(2)}) collective-permute-start(bf16[512,256]{1,0:T(8,128)(2,1)S(1)} %get-tuple-element.111), channel_id=1, source_target_pairs={{0,1},{1,0},{2,3},{3,2},{4,5},{5,4},{6,7},{7,6},{8,9},{9,8},{10,11... | collective-permute-start | bytes 786440 | tf_op jit(solution)/shard_map/ppermute | solution.py:200
  43.1 4.0 %shard_map.88 = (bf16[256,256]{1,0:T(8,128)(2,1)S(1)}, bf16[256,256]{1,0:T(8,128)(2,1)S(1)}, bf16[256,256]{1,0:T(8,128)(2,1)S(1)}, bf16[256,256]{1,0:T(8,128)(2,...) custom-call(s32[2]{0:T(128)S(1)} %pad_add_fusion.place, ...), custom_call_target="tpu_custom_call" | custom-call | tf_op jit(solution)/shard_map/pallas_call | solution.py:141
  47.2 0.7 %collective-permute-start.12 = (bf16[512,256]{1,0:T(8,128)(2,1)S(1)}, bf16[512,256]{1,0:T(8,128)(2,1)S(1)}, u32[]{:S(2)}, u32[]{:S(2)}) collective-permute-start(bf16[512,256]{1,0:T(8,128)(2,1)S(1)} %get-tuple-element.71), channel_id=1, source_target_pairs={{0,2},{2,0},{4,6},{6,4},{8,10},{10,8},{12,14},{14,12},{16,18},{18,... | collective-permute-start | bytes 786440 | tf_op jit(solution)/shard_map/ppermute | solution.py:195
  48.0 2.3 %collective-permute-start.15 = (bf16[2,512,256]{2,1,0:T(8,128)(2,1)S(1)}, bf16[2,512,256]{2,1,0:T(8,128)(2,1)S(1)}, u32[]{:S(2)}, u32[]{:S(2)}) collective-permute-start(bf16[2,512,256]{2,1,0:T(8,128)(2,1)S(1)} %pad_maximum_fusion.2), channel_id=1, source_target_pairs={{0,1},{1,0},{2,3},{3,2},{4,5},{5,4},{6,7},{7,6},{8,9},{9,8},{10,11... | collective-permute-start | bytes 1572872 | tf_op jit(solution)/shard_map/ppermute | solution.py:204
  50.4 0.2 fusion.11
  50.5 0.3 collective-permute-start.16
  50.9 0.7 %copy-done = bf16[512,1024]{1,0:T(8,128)(2,1)S(1)} copy-done((bf16[512,1024]{1,0:T(8,128)(2,1)S(1)}, bf16[512,1024]{1,0:T(8,128)(2,1)}, u32[]{:S(2)}) %copy-start) | copy-done | bytes 1048600
  51.6 4.0 %shard_map.89 = (bf16[256,256]{1,0:T(8,128)(2,1)S(1)}, bf16[256,256]{1,0:T(8,128)(2,1)S(1)}, bf16[256,256]{1,0:T(8,128)(2,1)S(1)}, bf16[256,256]{1,0:T(8,128)(2,...) custom-call(s32[2]{0:T(128)S(1)} %pad_add_fusion.place, ...), custom_call_target="tpu_custom_call" | custom-call | tf_op jit(solution)/shard_map/pallas_call | solution.py:141
  55.6 0.8 %collective-permute-start.14 = (bf16[512,256]{1,0:T(8,128)(2,1)S(1)}, bf16[512,256]{1,0:T(8,128)(2,1)S(1)}, u32[]{:S(2)}, u32[]{:S(2)}) collective-permute-start(bf16[512,256]{1,0:T(8,128)(2,1)S(1)} %get-tuple-element.92), channel_id=1, source_target_pairs={{0,2},{2,0},{4,6},{6,4},{8,10},{10,8},{12,14},{14,12},{16,18},{18,... | collective-permute-start | bytes 786440 | tf_op jit(solution)/shard_map/ppermute | solution.py:195
  56.6 0.9 %collective-permute-done.14 = bf16[512,256]{1,0:T(8,128)(2,1)S(1)} collective-permute-done((bf16[512,256]{1,0:T(8,128)(2,1)S(1)}, bf16[512,256]{1,0:T(8,128)(2,1)S(1)}, u32[]{:S(2)}, u32[]{:S(2)}) %collective-permute-start.14) | collective-permute-done | bytes 262176 | tf_op jit(solution)/shard_map/ppermute | solution.py:195
  57.8 1.1 %pad_maximum_fusion.1 = bf16[256,2048]{1,0:T(8,128)(2,1)} fusion(bf16[256,512]{1,0:T(8,128)(2,1)S(1)} %get-tuple-element.101, bf16[256,512]{1,0:T(8,128)(2,1)S(1)} %get-tuple-element.100, bf16[256,512]{1,0:T(8,128)(2,1)S(1)} %get-tuple-element.99, bf16[256,512]{1,0:T(8,128)(2,1)S(1)} %get-tuple-element.98), kind=kLoop, calls=%fused_computation.1 | loop fusion | flops 4194304 | bytes 2097152 | tf_op jit(solution)/shard_map/concatenate | solution.py:217
  58.9 1.1 %pad_maximum_fusion = bf16[256,2048]{1,0:T(8,128)(2,1)} fusion(bf16[256,512]{1,0:T(8,128)(2,1)S(1)} %get-tuple-element.105, bf16[256,512]{1,0:T(8,128)(2,1)S(1)} %get-tuple-element.104, bf16[256,512]{1,0:T(8,128)(2,1)S(1)} %get-tuple-element.103, bf16[256,512]{1,0:T(8,128)(2,1)S(1)} %get-tuple-element.102), kind=kLoop, calls=%fused_computation | loop fusion | flops 4194304 | bytes 2097152 | tf_op jit(solution)/shard_map/concatenate | solution.py:217
  60.0 3.3 %collective-permute-done.15.crossed = bf16[2,512,256]{2,1,0:T(8,128)(2,1)S(1)} collective-permute-done((bf16[2,512,256]{2,1,0:T(8,128)(2,1)S(1)}, bf16[2,512,256]{2,1,0:T(8,128)(2,1)S(1)}, u32[]{:S(2)}, u32[]{:S(2)}) %collective-permute-start.15) | collective-permute-done | bytes 524320 | tf_op jit(solution)/shard_map/ppermute | solution.py:204
  63.3 2.0 %collective-permute-done.18.arrived1 = bf16[512,256]{1,0:T(8,128)(2,1)S(1)} collective-permute-done((bf16[512,256]{1,0:T(8,128)(2,1)S(1)}, bf16[512,256]{1,0:T(8,128)(2,1)S(1)}, u32[]{:S(2)}, u32[]{:S(2)}) %collective-permute-start.18) | collective-permute-done | bytes 262176 | tf_op jit(solution)/shard_map/ppermute | solution.py:203
  65.3 0.9 %shard_map.90 = (bf16[256,512]{1,0:T(8,128)(2,1)}, bf16[256,512]{1,0:T(8,128)(2,1)}) custom-call(f32[512,256]{1,0:T(8,128)S(1)} %get-tuple-element.112.near0, f32[512,256]{1,0:T(8,128)S(1)} %get-tuple-element.107.near1, bf16[2,512,256]{2,1,0:T(8,128)(2,1)S(1)} %collective-permute-done.15.crossed, bf16[512,256]{1,0:T(8,128)(2,1)S(1)} %collective-permute-done.16.arrived0, ...), custom_call_target="tpu_custom_call" | custom-call | tf_op jit(solution)/shard_map/pallas_call | solution.py:205
  (49 shorter events, 1.3 us)
Async XLA Ops:
  0.7 1.9 %copy-start.4 = (bf16[256,1024]{1,0:T(8,128)(2,1)S(1)}, bf16[256,1024]{1,0:T(8,128)(2,1)}, u32[]{:S(2)}) copy-start(bf16[256,1024]{1,0:T(8,128)(2,1)} %refs_28_.1) | copy-start | bytes 1572868
  0.7 5.3 %copy-start.5 = (bf16[256,1024]{1,0:T(8,128)(2,1)S(1)}, bf16[256,1024]{1,0:T(8,128)(2,1)}, u32[]{:S(2)}) copy-start(bf16[256,1024]{1,0:T(8,128)(2,1)} %refs_29_.1) | copy-start | bytes 1572868
  2.6 19.1 %copy-start.3 = (s32[128]{0:T(128)S(1)}, s32[128]{0:T(128)}, u32[]{:S(2)}) copy-start(s32[128]{0:T(128)} %order.7) | copy-start | bytes 1540
  2.6 4.9 %collective-permute-start = (bf16[256,1024]{1,0:T(8,128)(2,1)S(1)}, bf16[256,1024]{1,0:T(8,128)(2,1)S(1)}, u32[]{:S(2)}, u32[]{:S(2)}) collective-permute-start(bf16[256,1024]{1,0:T(8,128)(2,1)S(1)} %copy-done.4), channel_id=1, source_target_pairs={{0,2},{2,0},{4,6},{6,4},{8,10},{10,8},{12,14},{14,12},{16,18},{18,... | collective-permute-start | bytes 1572872 | tf_op jit(solution)/shard_map/ppermute | solution.py:176
  6.0 2.3 %collective-permute-start.1 = (bf16[256,1024]{1,0:T(8,128)(2,1)S(1)}, bf16[256,1024]{1,0:T(8,128)(2,1)S(1)}, u32[]{:S(2)}, u32[]{:S(2)}) collective-permute-start(bf16[256,1024]{1,0:T(8,128)(2,1)S(1)} %copy-done.5), channel_id=1, source_target_pairs={{0,2},{2,0},{4,6},{6,4},{8,10},{10,8},{12,14},{14,12},{16,18},{18,... | collective-permute-start | bytes 1572872 | tf_op jit(solution)/shard_map/ppermute | solution.py:177
  6.1 13.6 %collective-permute-start.4 = (bf16[512,256]{1,0:T(8,128)(2,1)S(1)}, bf16[512,256]{1,0:T(8,128)(2,1)S(1)}, u32[]{:S(2)}, u32[]{:S(2)}) collective-permute-start(bf16[512,256]{1,0:T(8,128)(2,1)S(1)} %get-tuple-element.51), channel_id=1, source_target_pairs={{0,4},{2,6},{4,8},{6,10},{8,12},{10,14},{12,16},{14,18},{16,20},{1... | collective-permute-start | bytes 786440 | tf_op jit(solution)/shard_map/ppermute | solution.py:174
  19.6 2.1 %collective-permute-start.5 = (bf16[512,256]{1,0:T(8,128)(2,1)S(1)}, bf16[512,256]{1,0:T(8,128)(2,1)S(1)}, u32[]{:S(2)}, u32[]{:S(2)}) collective-permute-start(bf16[512,256]{1,0:T(8,128)(2,1)S(1)} %collective-permute-done.4.far2), channel_id=1, source_target_pairs={{0,2},{2,0},{4,6},{6,4},{8,10},{10,8},{12,14},{14,12},{16,18},{18,... | collective-permute-start | bytes 786440 | tf_op jit(solution)/shard_map/ppermute | solution.py:188
  20.6 12.2 %collective-permute-start.3 = (bf16[512,256]{1,0:T(8,128)(2,1)S(1)}, bf16[512,256]{1,0:T(8,128)(2,1)S(1)}, u32[]{:S(2)}, u32[]{:S(2)}) collective-permute-start(bf16[512,256]{1,0:T(8,128)(2,1)S(1)} %get-tuple-element.57), channel_id=1, source_target_pairs={{0,4},{2,6},{4,8},{6,10},{8,12},{10,14},{12,16},{14,18},{16,20},{1... | collective-permute-start | bytes 786440 | tf_op jit(solution)/shard_map/ppermute | solution.py:174
  25.8 7.8 %collective-permute-start.7 = (bf16[512,256]{1,0:T(8,128)(2,1)S(1)}, bf16[512,256]{1,0:T(8,128)(2,1)S(1)}, u32[]{:S(2)}, u32[]{:S(2)}) collective-permute-start(bf16[512,256]{1,0:T(8,128)(2,1)S(1)} %get-tuple-element.60), channel_id=1, source_target_pairs={{0,2},{2,0},{4,6},{6,4},{8,10},{10,8},{12,14},{14,12},{16,18},{18,... | collective-permute-start | bytes 786440 | tf_op jit(solution)/shard_map/ppermute | solution.py:195
  26.2 14.6 %collective-permute-start.2 = (bf16[512,256]{1,0:T(8,128)(2,1)S(1)}, bf16[512,256]{1,0:T(8,128)(2,1)S(1)}, u32[]{:S(2)}, u32[]{:S(2)}) collective-permute-start(bf16[512,256]{1,0:T(8,128)(2,1)S(1)} %get-tuple-element.55), channel_id=1, source_target_pairs={{0,4},{2,6},{4,8},{6,10},{8,12},{10,14},{12,16},{14,18},{16,20},{1... | collective-permute-start | bytes 786440 | tf_op jit(solution)/shard_map/ppermute | solution.py:174
  26.2 21.6 %collective-permute-start.10 = (bf16[512,256]{1,0:T(8,128)(2,1)S(1)}, bf16[512,256]{1,0:T(8,128)(2,1)S(1)}, u32[]{:S(2)}, u32[]{:S(2)}) collective-permute-start(bf16[512,256]{1,0:T(8,128)(2,1)S(1)} %get-tuple-element.70), channel_id=1, source_target_pairs={{0,4},{2,6},{4,8},{6,10},{8,12},{10,14},{12,16},{14,18},{16,20},{1... | collective-permute-start | bytes 786440 | tf_op jit(solution)/shard_map/ppermute | solution.py:174
  32.7 3.7 %collective-permute-start.6 = (bf16[512,256]{1,0:T(8,128)(2,1)S(1)}, bf16[512,256]{1,0:T(8,128)(2,1)S(1)}, u32[]{:S(2)}, u32[]{:S(2)}) collective-permute-start(bf16[512,256]{1,0:T(8,128)(2,1)S(1)} %collective-permute-done.3.far2), channel_id=1, source_target_pairs={{0,2},{2,0},{4,6},{6,4},{8,10},{10,8},{12,14},{14,12},{16,18},{18,... | collective-permute-start | bytes 786440 | tf_op jit(solution)/shard_map/ppermute | solution.py:188
  33.5 2.9 %copy-start.2 = (bf16[512,1024]{1,0:T(8,128)(2,1)S(1)}, bf16[512,1024]{1,0:T(8,128)(2,1)}, u32[]{:S(2)}) copy-start(bf16[512,1024]{1,0:T(8,128)(2,1)} %get-tuple-element.56.heads) | copy-start | bytes 3145732
  33.7 16.6 %collective-permute-start.13 = (bf16[512,256]{1,0:T(8,128)(2,1)S(1)}, bf16[512,256]{1,0:T(8,128)(2,1)S(1)}, u32[]{:S(2)}, u32[]{:S(2)}) collective-permute-start(bf16[512,256]{1,0:T(8,128)(2,1)S(1)} %get-tuple-element.109), channel_id=1, source_target_pairs={{0,1},{1,0},{2,3},{3,2},{4,5},{5,4},{6,7},{7,6},{8,9},{9,8},{10,11... | collective-permute-start | bytes 786440 | tf_op jit(solution)/shard_map/ppermute | solution.py:200
  40.5 1.6 %collective-permute-start.9 = (bf16[512,256]{1,0:T(8,128)(2,1)S(1)}, bf16[512,256]{1,0:T(8,128)(2,1)S(1)}, u32[]{:S(2)}, u32[]{:S(2)}) collective-permute-start(bf16[512,256]{1,0:T(8,128)(2,1)S(1)} %get-tuple-element.64), channel_id=1, source_target_pairs={{0,2},{2,0},{4,6},{6,4},{8,10},{10,8},{12,14},{14,12},{16,18},{18,... | collective-permute-start | bytes 786440 | tf_op jit(solution)/shard_map/ppermute | solution.py:195
  40.9 2.2 %collective-permute-start.8 = (bf16[512,256]{1,0:T(8,128)(2,1)S(1)}, bf16[512,256]{1,0:T(8,128)(2,1)S(1)}, u32[]{:S(2)}, u32[]{:S(2)}) collective-permute-start(bf16[512,256]{1,0:T(8,128)(2,1)S(1)} %collective-permute-done.2.far2), channel_id=1, source_target_pairs={{0,2},{2,0},{4,6},{6,4},{8,10},{10,8},{12,14},{14,12},{16,18},{18,... | collective-permute-start | bytes 786440 | tf_op jit(solution)/shard_map/ppermute | solution.py:188
  41.1 2.0 %copy-start.1 = (bf16[512,1024]{1,0:T(8,128)(2,1)S(1)}, bf16[512,1024]{1,0:T(8,128)(2,1)}, u32[]{:S(2)}) copy-start(bf16[512,1024]{1,0:T(8,128)(2,1)} %get-tuple-element.54.heads) | copy-start | bytes 3145732
  42.3 14.3 %collective-permute-start.17 = (bf16[512,256]{1,0:T(8,128)(2,1)S(1)}, bf16[512,256]{1,0:T(8,128)(2,1)S(1)}, u32[]{:S(2)}, u32[]{:S(2)}) collective-permute-start(bf16[512,256]{1,0:T(8,128)(2,1)S(1)} %get-tuple-element.111), channel_id=1, source_target_pairs={{0,1},{1,0},{2,3},{3,2},{4,5},{5,4},{6,7},{7,6},{8,9},{9,8},{10,11... | collective-permute-start | bytes 786440 | tf_op jit(solution)/shard_map/ppermute | solution.py:200
  47.2 3.2 %collective-permute-start.12 = (bf16[512,256]{1,0:T(8,128)(2,1)S(1)}, bf16[512,256]{1,0:T(8,128)(2,1)S(1)}, u32[]{:S(2)}, u32[]{:S(2)}) collective-permute-start(bf16[512,256]{1,0:T(8,128)(2,1)S(1)} %get-tuple-element.71), channel_id=1, source_target_pairs={{0,2},{2,0},{4,6},{6,4},{8,10},{10,8},{12,14},{14,12},{16,18},{18,... | collective-permute-start | bytes 786440 | tf_op jit(solution)/shard_map/ppermute | solution.py:195
  47.8 3.0 %collective-permute-start.11 = (bf16[512,256]{1,0:T(8,128)(2,1)S(1)}, bf16[512,256]{1,0:T(8,128)(2,1)S(1)}, u32[]{:S(2)}, u32[]{:S(2)}) collective-permute-start(bf16[512,256]{1,0:T(8,128)(2,1)S(1)} %collective-permute-done.10.far2), channel_id=1, source_target_pairs={{0,2},{2,0},{4,6},{6,4},{8,10},{10,8},{12,14},{14,12},{16,18},{18,... | collective-permute-start | bytes 786440 | tf_op jit(solution)/shard_map/ppermute | solution.py:188
  48.0 15.3 %collective-permute-start.15 = (bf16[2,512,256]{2,1,0:T(8,128)(2,1)S(1)}, bf16[2,512,256]{2,1,0:T(8,128)(2,1)S(1)}, u32[]{:S(2)}, u32[]{:S(2)}) collective-permute-start(bf16[2,512,256]{2,1,0:T(8,128)(2,1)S(1)} %pad_maximum_fusion.2), channel_id=1, source_target_pairs={{0,1},{1,0},{2,3},{3,2},{4,5},{5,4},{6,7},{7,6},{8,9},{9,8},{10,11... | collective-permute-start | bytes 1572872 | tf_op jit(solution)/shard_map/ppermute | solution.py:204
  50.3 1.2 %copy-start = (bf16[512,1024]{1,0:T(8,128)(2,1)S(1)}, bf16[512,1024]{1,0:T(8,128)(2,1)}, u32[]{:S(2)}) copy-start(bf16[512,1024]{1,0:T(8,128)(2,1)} %get-tuple-element.69.heads) | copy-start | bytes 3145732
  50.5 12.8 %collective-permute-start.16 = (bf16[512,256]{1,0:T(8,128)(2,1)S(1)}, bf16[512,256]{1,0:T(8,128)(2,1)S(1)}, u32[]{:S(2)}, u32[]{:S(2)}) collective-permute-start(bf16[512,256]{1,0:T(8,128)(2,1)S(1)} %get-tuple-element.113), channel_id=1, source_target_pairs={{4,0},{6,2},{8,4},{10,6},{12,8},{14,10},{16,12},{18,14},{20,16},{2... | collective-permute-start | bytes 786440 | tf_op jit(solution)/shard_map/ppermute | solution.py:203
  55.6 1.9 %collective-permute-start.14 = (bf16[512,256]{1,0:T(8,128)(2,1)S(1)}, bf16[512,256]{1,0:T(8,128)(2,1)S(1)}, u32[]{:S(2)}, u32[]{:S(2)}) collective-permute-start(bf16[512,256]{1,0:T(8,128)(2,1)S(1)} %get-tuple-element.92), channel_id=1, source_target_pairs={{0,2},{2,0},{4,6},{6,4},{8,10},{10,8},{12,14},{14,12},{16,18},{18,... | collective-permute-start | bytes 786440 | tf_op jit(solution)/shard_map/ppermute | solution.py:195
  57.7 7.6 %collective-permute-start.18 = (bf16[512,256]{1,0:T(8,128)(2,1)S(1)}, bf16[512,256]{1,0:T(8,128)(2,1)S(1)}, u32[]{:S(2)}, u32[]{:S(2)}) collective-permute-start(bf16[512,256]{1,0:T(8,128)(2,1)S(1)} %get-tuple-element.106), channel_id=1, source_target_pairs={{4,0},{6,2},{8,4},{10,6},{12,8},{14,10},{16,12},{18,14},{20,16},{2... | collective-permute-start | bytes 786440 | tf_op jit(solution)/shard_map/ppermute | solution.py:203

commit v4 on v3

--- a/solution.py
+++ b/solution.py
@@ -20,7 +20,7 @@
 
 
 def pack(place, *refs):
-    ins, outs = refs[: 2 * UNITS], refs[2 * UNITS :]
+    ins, outs = refs[:2], refs[2:]
     rows = ins[0].shape[0]
     for u, out in enumerate(outs):
         out[:rows, :] = ins[2 * u][...]
@@ -28,12 +28,15 @@
 
 
 def stage(place, *refs):
-    ins, outs = refs[: 8 * UNITS], refs[8 * UNITS :]
+    ins, outs, packed = refs[: 8 * UNITS], refs[8 * UNITS : 9 * UNITS], refs[9 * UNITS :]
     rows, width = ins[0].shape
     for u, out in enumerate(outs):
         for n in range(8):
             at = slice(n // 2 * width, (n // 2 + 1) * width)
             out[n % 2 * rows : (n % 2 + 1) * rows, at] = ins[8 * u + n][...]
+        if u:
+            packed[u - 1][:rows, :] = ins[8 * u + 4][...]
+            packed[u - 1][rows:, :] = ins[8 * u + 5][...]
 
 
 def finish(near0, near1, crossed, arrived0, arrived1, key_grad, value_grad):
@@ -95,7 +98,7 @@
 def pack_units(place, keys, values):
     rows, width = keys.shape[0], keys.shape[1] // UNITS
     specs = []
-    for u in range(UNITS):
+    for u in range(1):
         specs += [pl.BlockSpec((rows, width), lambda t, place, u=u: (0, unit_at(u, place)))] * 2
     return pl.pallas_call(
         pack,
@@ -103,12 +106,12 @@
             num_scalar_prefetch=1,
             grid=(1,),
             in_specs=specs,
-            out_specs=[pl.BlockSpec((2 * rows, width), lambda t, place: (0, 0))] * UNITS,
+            out_specs=[pl.BlockSpec((2 * rows, width), lambda t, place: (0, 0))] * 1,
         ),
-        out_shape=[jax.ShapeDtypeStruct((2 * rows, width), keys.dtype)] * UNITS,
+        out_shape=[jax.ShapeDtypeStruct((2 * rows, width), keys.dtype)] * 1,
         compiler_params=pltpu.CompilerParams(vmem_limit_bytes=VMEM_LIMIT),
         cost_estimate=pl.CostEstimate(flops=0, bytes_accessed=8 * keys.size, transcendentals=0),
-    )(place, *([keys, values] * UNITS))
+    )(place, keys, values)
 
 
 def stage_heads(place, queries, out_grad, keys, values, near_keys, near_values, width):
@@ -125,9 +128,11 @@
             num_scalar_prefetch=1,
             grid=(1,),
             in_specs=specs,
-            out_specs=[pl.BlockSpec(shape, lambda t, place: (0, 0))] * UNITS,
+            out_specs=[pl.BlockSpec(shape, lambda t, place: (0, 0))] * UNITS
+            + [pl.BlockSpec((2 * rows, width), lambda t, place: (0, 0))] * (UNITS - 1),
         ),
-        out_shape=[jax.ShapeDtypeStruct(shape, queries.dtype)] + [pltpu.HBM(shape, queries.dtype)] * (UNITS - 1),
+        out_shape=[jax.ShapeDtypeStruct(shape, queries.dtype)] + [pltpu.HBM(shape, queries.dtype)] * (UNITS - 1)
+        + [jax.ShapeDtypeStruct((2 * rows, width), keys.dtype)] * (UNITS - 1),
         compiler_params=pltpu.CompilerParams(vmem_limit_bytes=VMEM_LIMIT),
     )(place, *([queries, queries, out_grad, out_grad, keys, values, near_keys, near_values] * UNITS))
 
@@ -171,13 +176,15 @@
     ]
 
     own = pack_units(place, keys, values)
-    far2 = [lax.ppermute(x, "cp", ahead) for x in own]
+    far2 = [lax.ppermute(own[0], "cp", ahead)]
     raw_keys, raw_values, _ = lax.optimization_barrier((raw_keys, raw_values, own[0]))
     near_keys = lax.ppermute(raw_keys, "cp", swap)
     near_values = lax.ppermute(raw_values, "cp", swap)
-    heads = stage_heads(
+    staged = stage_heads(
         place, queries, out_grad, keys, values, near_keys, near_values, own[0].shape[1]
     )
+    heads = staged[:UNITS]
+    far2 += [lax.ppermute(x, "cp", ahead) for x in staged[UNITS:]]
     far2[0], _ = lax.optimization_barrier((far2[0], heads[0]))
     results, near, arrived = [], [], []
     crossed = []

time: 66.4 us -> 66 us (level)
  no operation moved by 1% of the time
where the time goes in v4:
time: 66 us; the launch traced here: 65.9 us
  waiting for transfers between devices  23.9 us (36%)
  Pallas kernels  23.1 us (35%)
  starting transfers between devices  14 us (21%)
  other arithmetic  3.14 us (5%)
  between operations  0.91 us (1%)
  local copies, waits for them, and re-layouts  0.89 us (1%)
    pallas_call x4, Pallas kernels, attend_unit(): pl.pallas_call(attend, grid_spec=pltpu.PrefetchScalarGridSpec(num_scalar_...  16.1 us
    ppermute x1, waiting for transfers between devices, on_device(): far2 = [lax.ppermute(own[0], 'cp', ahead)]  6.91 us
    ppermute x3, waiting for transfers between devices, on_device(): far2 += [lax.ppermute(x, 'cp', ahead) for x in staged[UNITS:]]  6.49 us
    pallas_call x1, Pallas kernels, stage_heads(): pl.pallas_call(stage, grid_spec=pltpu.PrefetchScalarGridSpec(num_scalar_p...  4.46 us
    ppermute x2, starting transfers between devices, on_device(): crossed.append(lax.ppermute(send, 'kv', across))  3.56 us
    ppermute x1, starting transfers between devices, on_device(): near_keys = lax.ppermute(raw_keys, 'cp', swap)  3.33 us
    ppermute x1, waiting for transfers between devices, on_device(): lax.ppermute(jnp.stack([near[0], near[1]]).astype(bf16), 'kv', across)  3.32 us
    ppermute x1, starting transfers between devices, on_device(): lax.ppermute(jnp.stack([near[0], near[1]]).astype(bf16), 'kv', across)  2.3 us
  transfers between devices with their start and end apart: 19, of which 9 were waited for; matrix products, arithmetic and copies ran while one was open for 5% of the time, Pallas kernels for 31%

profile of v4, /device:TPU:1, one launch (start us, length us, event | category | flops | bytes accessed | tf_op | source)
XLA Modules:
  0.0 65.9 jit_solution(7248383073651713650)
XLA Ops:
  0.7 1.5 %shard_map.84 = bf16[512,256]{1,0:T(8,128)(2,1)S(1)} custom-call(s32[2]{0:T(128)S(1)} %pad_add_fusion.place, bf16[256,1024]{1,0:T(8,128)(2,1)} %refs_28_.1, bf16[256,1024]{1,0:T(8,128)(2,1)} %refs_29_.1), custom_call_target="tpu_custom_call" | custom-call | bytes 2097152 | tf_op jit(solution)/shard_map/pallas_call | solution.py:103
  2.3 3.3 %collective-permute-start = (bf16[256,1024]{1,0:T(8,128)(2,1)S(1)}, bf16[256,1024]{1,0:T(8,128)(2,1)S(1)}, u32[]{:S(2)}, u32[]{:S(2)}) collective-permute-start(bf16[256,1024]{1,0:T(8,128)(2,1)S(1)} %copy-done.4), channel_id=1, source_target_pairs={{0,2},{2,0},{4,6},{6,4},{8,10},{10,8},{12,14},{14,12},{16,18},{18,... | collective-permute-start | bytes 1572872 | tf_op jit(solution)/shard_map/ppermute | solution.py:181
  5.7 1.4 %collective-permute-done.refs_6_.refs_14_.refs_22_.refs_30_ = bf16[256,1024]{1,0:T(8,128)(2,1)S(1)} collective-permute-done((bf16[256,1024]{1,0:T(8,128)(2,1)S(1)}, bf16[256,1024]{1,0:T(8,128)(2,1)S(1)}, u32[]{:S(2)}, u32[]{:S(2)}) %collective-permute-start) | collective-permute-done | bytes 524320 | tf_op jit(solution)/shard_map/ppermute | solution.py:181
  7.2 0.7 %collective-permute-done.1.refs_7_.refs_15_.refs_23_.refs_31_ = bf16[256,1024]{1,0:T(8,128)(2,1)S(1)} collective-permute-done((bf16[256,1024]{1,0:T(8,128)(2,1)S(1)}, bf16[256,1024]{1,0:T(8,128)(2,1)S(1)}, u32[]{:S(2)}, u32[]{:S(2)}) %collective-permute-start.1) | collective-permute-done | bytes 524320 | tf_op jit(solution)/shard_map/ppermute | solution.py:182
  7.9 4.5 %shard_map.85 = (bf16[512,1024]{1,0:T(8,128)(2,1)S(1)}, bf16[512,1024]{1,0:T(8,128)(2,1)}, bf16[512,1024]{1,0:T(8,128)(2,1)}, bf16[512,1024]{1,0:T(8,128)(2,1)},...) custom-call(s32[2]{0:T(128)S(1)} %pad_add_fusion.place, ...), custom_call_target="tpu_custom_call" | custom-call | tf_op jit(solution)/shard_map/pallas_call | solution.py:125
  12.4 6.9 %collective-permute-done.4.far2 = bf16[512,256]{1,0:T(8,128)(2,1)S(1)} collective-permute-done((bf16[512,256]{1,0:T(8,128)(2,1)S(1)}, bf16[512,256]{1,0:T(8,128)(2,1)S(1)}, u32[]{:S(2)}, u32[]{:S(2)}) %collective-permute-start.4) | collective-permute-done | bytes 262176 | tf_op jit(solution)/shard_map/ppermute | solution.py:179
  19.3 0.9 %collective-permute-start.5 = (bf16[512,256]{1,0:T(8,128)(2,1)S(1)}, bf16[512,256]{1,0:T(8,128)(2,1)S(1)}, u32[]{:S(2)}, u32[]{:S(2)}) collective-permute-start(bf16[512,256]{1,0:T(8,128)(2,1)S(1)} %collective-permute-done.4.far2), channel_id=1, source_target_pairs={{0,2},{2,0},{4,6},{6,4},{8,10},{10,8},{12,14},{14,12},{16,18},{18,... | collective-permute-start | bytes 786440 | tf_op jit(solution)/shard_map/ppermute | solution.py:195
  20.2 1.2 %collective-permute-done.5.far1 = bf16[512,256]{1,0:T(8,128)(2,1)S(1)} collective-permute-done((bf16[512,256]{1,0:T(8,128)(2,1)S(1)}, bf16[512,256]{1,0:T(8,128)(2,1)S(1)}, u32[]{:S(2)}, u32[]{:S(2)}) %collective-permute-start.5) | collective-permute-done | bytes 262176 | tf_op jit(solution)/shard_map/ppermute | solution.py:195
  21.4 4.0 %shard_map.86 = (bf16[256,256]{1,0:T(8,128)(2,1)S(1)}, bf16[256,256]{1,0:T(8,128)(2,1)S(1)}, bf16[256,256]{1,0:T(8,128)(2,1)S(1)}, bf16[256,256]{1,0:T(8,128)(2,...) custom-call(s32[2]{0:T(128)S(1)} %pad_add_fusion.place, ...), custom_call_target="tpu_custom_call" | custom-call | tf_op jit(solution)/shard_map/pallas_call | solution.py:146
  25.4 0.5 collective-permute-start.7
  25.9 6.5 %collective-permute-done.3.far2 = bf16[512,256]{1,0:T(8,128)(2,1)S(1)} collective-permute-done((bf16[512,256]{1,0:T(8,128)(2,1)S(1)}, bf16[512,256]{1,0:T(8,128)(2,1)S(1)}, u32[]{:S(2)}, u32[]{:S(2)}) %collective-permute-start.3) | collective-permute-done | bytes 262176 | tf_op jit(solution)/shard_map/ppermute | solution.py:187
  32.4 0.8 %collective-permute-start.6 = (bf16[512,256]{1,0:T(8,128)(2,1)S(1)}, bf16[512,256]{1,0:T(8,128)(2,1)S(1)}, u32[]{:S(2)}, u32[]{:S(2)}) collective-permute-start(bf16[512,256]{1,0:T(8,128)(2,1)S(1)} %collective-permute-done.3.far2), channel_id=1, source_target_pairs={{0,2},{2,0},{4,6},{6,4},{8,10},{10,8},{12,14},{14,12},{16,18},{18,... | collective-permute-start | bytes 786440 | tf_op jit(solution)/shard_map/ppermute | solution.py:195
  33.4 2.7 %collective-permute-start.13 = (bf16[512,256]{1,0:T(8,128)(2,1)S(1)}, bf16[512,256]{1,0:T(8,128)(2,1)S(1)}, u32[]{:S(2)}, u32[]{:S(2)}) collective-permute-start(bf16[512,256]{1,0:T(8,128)(2,1)S(1)} %get-tuple-element.107), channel_id=1, source_target_pairs={{0,1},{1,0},{2,3},{3,2},{4,5},{5,4},{6,7},{7,6},{8,9},{9,8},{10,11... | collective-permute-start | bytes 786440 | tf_op jit(solution)/shard_map/ppermute | solution.py:207
  36.1 4.0 %shard_map.87 = (bf16[256,256]{1,0:T(8,128)(2,1)S(1)}, bf16[256,256]{1,0:T(8,128)(2,1)S(1)}, bf16[256,256]{1,0:T(8,128)(2,1)S(1)}, bf16[256,256]{1,0:T(8,128)(2,...) custom-call(s32[2]{0:T(128)S(1)} %pad_add_fusion.place, ...), custom_call_target="tpu_custom_call" | custom-call | tf_op jit(solution)/shard_map/pallas_call | solution.py:146
  40.1 0.4 collective-permute-start.9
  40.5 0.2 collective-permute-start.8
  40.8 0.9 %collective-permute-done.9 = bf16[512,256]{1,0:T(8,128)(2,1)S(1)} collective-permute-done((bf16[512,256]{1,0:T(8,128)(2,1)S(1)}, bf16[512,256]{1,0:T(8,128)(2,1)S(1)}, u32[]{:S(2)}, u32[]{:S(2)}) %collective-permute-start.9) | collective-permute-done | bytes 262176 | tf_op jit(solution)/shard_map/ppermute | solution.py:202
  41.9 0.8 %collective-permute-start.17 = (bf16[512,256]{1,0:T(8,128)(2,1)S(1)}, bf16[512,256]{1,0:T(8,128)(2,1)S(1)}, u32[]{:S(2)}, u32[]{:S(2)}) collective-permute-start(bf16[512,256]{1,0:T(8,128)(2,1)S(1)} %get-tuple-element.109), channel_id=1, source_target_pairs={{0,1},{1,0},{2,3},{3,2},{4,5},{5,4},{6,7},{7,6},{8,9},{9,8},{10,11... | collective-permute-start | bytes 786440 | tf_op jit(solution)/shard_map/ppermute | solution.py:207
  42.8 4.0 %shard_map.88 = (bf16[256,256]{1,0:T(8,128)(2,1)S(1)}, bf16[256,256]{1,0:T(8,128)(2,1)S(1)}, bf16[256,256]{1,0:T(8,128)(2,1)S(1)}, bf16[256,256]{1,0:T(8,128)(2,...) custom-call(s32[2]{0:T(128)S(1)} %pad_add_fusion.place, ...), custom_call_target="tpu_custom_call" | custom-call | tf_op jit(solution)/shard_map/pallas_call | solution.py:146
  46.8 0.6 collective-permute-start.12
  47.6 2.3 %collective-permute-start.15 = (bf16[2,512,256]{2,1,0:T(8,128)(2,1)S(1)}, bf16[2,512,256]{2,1,0:T(8,128)(2,1)S(1)}, u32[]{:S(2)}, u32[]{:S(2)}) collective-permute-start(bf16[2,512,256]{2,1,0:T(8,128)(2,1)S(1)} %pad_maximum_fusion.2), channel_id=1, source_target_pairs={{0,1},{1,0},{2,3},{3,2},{4,5},{5,4},{6,7},{7,6},{8,9},{9,8},{10,11... | collective-permute-start | bytes 1572872 | tf_op jit(solution)/shard_map/ppermute | solution.py:211
  50.0 0.2 fusion.11
  50.2 0.3 collective-permute-start.16
  50.5 0.7 %copy-done = bf16[512,1024]{1,0:T(8,128)(2,1)S(1)} copy-done((bf16[512,1024]{1,0:T(8,128)(2,1)S(1)}, bf16[512,1024]{1,0:T(8,128)(2,1)}, u32[]{:S(2)}) %copy-start) | copy-done | bytes 1048600
  51.2 4.0 %shard_map.89 = (bf16[256,256]{1,0:T(8,128)(2,1)S(1)}, bf16[256,256]{1,0:T(8,128)(2,1)S(1)}, bf16[256,256]{1,0:T(8,128)(2,1)S(1)}, bf16[256,256]{1,0:T(8,128)(2,...) custom-call(s32[2]{0:T(128)S(1)} %pad_add_fusion.place, ...), custom_call_target="tpu_custom_call" | custom-call | tf_op jit(solution)/shard_map/pallas_call | solution.py:146
  55.2 0.8 %collective-permute-start.14 = (bf16[512,256]{1,0:T(8,128)(2,1)S(1)}, bf16[512,256]{1,0:T(8,128)(2,1)S(1)}, u32[]{:S(2)}, u32[]{:S(2)}) collective-permute-start(bf16[512,256]{1,0:T(8,128)(2,1)S(1)} %get-tuple-element.90), channel_id=1, source_target_pairs={{0,2},{2,0},{4,6},{6,4},{8,10},{10,8},{12,14},{14,12},{16,18},{18,... | collective-permute-start | bytes 786440 | tf_op jit(solution)/shard_map/ppermute | solution.py:202
  56.3 0.9 %collective-permute-done.14 = bf16[512,256]{1,0:T(8,128)(2,1)S(1)} collective-permute-done((bf16[512,256]{1,0:T(8,128)(2,1)S(1)}, bf16[512,256]{1,0:T(8,128)(2,1)S(1)}, u32[]{:S(2)}, u32[]{:S(2)}) %collective-permute-start.14) | collective-permute-done | bytes 262176 | tf_op jit(solution)/shard_map/ppermute | solution.py:202
  57.4 1.1 %pad_maximum_fusion.1 = bf16[256,2048]{1,0:T(8,128)(2,1)} fusion(bf16[256,512]{1,0:T(8,128)(2,1)S(1)} %get-tuple-element.99, bf16[256,512]{1,0:T(8,128)(2,1)S(1)} %get-tuple-element.98, bf16[256,512]{1,0:T(8,128)(2,1)S(1)} %get-tuple-element.97, bf16[256,512]{1,0:T(8,128)(2,1)S(1)} %get-tuple-element.96), kind=kLoop, calls=%fused_computation.1 | loop fusion | flops 4194304 | bytes 2097152 | tf_op jit(solution)/shard_map/concatenate | solution.py:224
  58.5 1.1 %pad_maximum_fusion = bf16[256,2048]{1,0:T(8,128)(2,1)} fusion(bf16[256,512]{1,0:T(8,128)(2,1)S(1)} %get-tuple-element.103, bf16[256,512]{1,0:T(8,128)(2,1)S(1)} %get-tuple-element.102, bf16[256,512]{1,0:T(8,128)(2,1)S(1)} %get-tuple-element.101, bf16[256,512]{1,0:T(8,128)(2,1)S(1)} %get-tuple-element.100), kind=kLoop, calls=%fused_computation | loop fusion | flops 4194304 | bytes 2097152 | tf_op jit(solution)/shard_map/concatenate | solution.py:224
  59.6 3.3 %collective-permute-done.15.crossed = bf16[2,512,256]{2,1,0:T(8,128)(2,1)S(1)} collective-permute-done((bf16[2,512,256]{2,1,0:T(8,128)(2,1)S(1)}, bf16[2,512,256]{2,1,0:T(8,128)(2,1)S(1)}, u32[]{:S(2)}, u32[]{:S(2)}) %collective-permute-start.15) | collective-permute-done | bytes 524320 | tf_op jit(solution)/shard_map/ppermute | solution.py:211
  63.0 2.0 %collective-permute-done.18.arrived1 = bf16[512,256]{1,0:T(8,128)(2,1)S(1)} collective-permute-done((bf16[512,256]{1,0:T(8,128)(2,1)S(1)}, bf16[512,256]{1,0:T(8,128)(2,1)S(1)}, u32[]{:S(2)}, u32[]{:S(2)}) %collective-permute-start.18) | collective-permute-done | bytes 262176 | tf_op jit(solution)/shard_map/ppermute | solution.py:210
  64.9 0.9 %shard_map.90 = (bf16[256,512]{1,0:T(8,128)(2,1)}, bf16[256,512]{1,0:T(8,128)(2,1)}) custom-call(f32[512,256]{1,0:T(8,128)S(1)} %get-tuple-element.110.near0, f32[512,256]{1,0:T(8,128)S(1)} %get-tuple-element.105.near1, bf16[2,512,256]{2,1,0:T(8,128)(2,1)S(1)} %collective-permute-done.15.crossed, bf16[512,256]{1,0:T(8,128)(2,1)S(1)} %collective-permute-done.16.arrived0, ...), custom_call_target="tpu_custom_call" | custom-call | tf_op jit(solution)/shard_map/pallas_call | solution.py:212
  (49 shorter events, 1.3 us)
Async XLA Ops:
  0.6 1.6 %copy-start.4 = (bf16[256,1024]{1,0:T(8,128)(2,1)S(1)}, bf16[256,1024]{1,0:T(8,128)(2,1)}, u32[]{:S(2)}) copy-start(bf16[256,1024]{1,0:T(8,128)(2,1)} %refs_28_.1) | copy-start | bytes 1572868
  0.6 5.0 %copy-start.5 = (bf16[256,1024]{1,0:T(8,128)(2,1)S(1)}, bf16[256,1024]{1,0:T(8,128)(2,1)}, u32[]{:S(2)}) copy-start(bf16[256,1024]{1,0:T(8,128)(2,1)} %refs_29_.1) | copy-start | bytes 1572868
  2.3 19.1 %copy-start.3 = (s32[128]{0:T(128)S(1)}, s32[128]{0:T(128)}, u32[]{:S(2)}) copy-start(s32[128]{0:T(128)} %order.7) | copy-start | bytes 1540
  2.3 4.9 %collective-permute-start = (bf16[256,1024]{1,0:T(8,128)(2,1)S(1)}, bf16[256,1024]{1,0:T(8,128)(2,1)S(1)}, u32[]{:S(2)}, u32[]{:S(2)}) collective-permute-start(bf16[256,1024]{1,0:T(8,128)(2,1)S(1)} %copy-done.4), channel_id=1, source_target_pairs={{0,2},{2,0},{4,6},{6,4},{8,10},{10,8},{12,14},{14,12},{16,18},{18,... | collective-permute-start | bytes 1572872 | tf_op jit(solution)/shard_map/ppermute | solution.py:181
  5.6 2.3 %collective-permute-start.1 = (bf16[256,1024]{1,0:T(8,128)(2,1)S(1)}, bf16[256,1024]{1,0:T(8,128)(2,1)S(1)}, u32[]{:S(2)}, u32[]{:S(2)}) collective-permute-start(bf16[256,1024]{1,0:T(8,128)(2,1)S(1)} %copy-done.5), channel_id=1, source_target_pairs={{0,2},{2,0},{4,6},{6,4},{8,10},{10,8},{12,14},{14,12},{16,18},{18,... | collective-permute-start | bytes 1572872 | tf_op jit(solution)/shard_map/ppermute | solution.py:182
  5.7 13.6 %collective-permute-start.4 = (bf16[512,256]{1,0:T(8,128)(2,1)S(1)}, bf16[512,256]{1,0:T(8,128)(2,1)S(1)}, u32[]{:S(2)}, u32[]{:S(2)}) collective-permute-start(bf16[512,256]{1,0:T(8,128)(2,1)S(1)} %shard_map.84), channel_id=1, source_target_pairs={{0,4},{2,6},{4,8},{6,10},{8,12},{10,14},{12,16},{14,18},{16,20},{1... | collective-permute-start | bytes 786440 | tf_op jit(solution)/shard_map/ppermute | solution.py:179
  19.3 2.1 %collective-permute-start.5 = (bf16[512,256]{1,0:T(8,128)(2,1)S(1)}, bf16[512,256]{1,0:T(8,128)(2,1)S(1)}, u32[]{:S(2)}, u32[]{:S(2)}) collective-permute-start(bf16[512,256]{1,0:T(8,128)(2,1)S(1)} %collective-permute-done.4.far2), channel_id=1, source_target_pairs={{0,2},{2,0},{4,6},{6,4},{8,10},{10,8},{12,14},{14,12},{16,18},{18,... | collective-permute-start | bytes 786440 | tf_op jit(solution)/shard_map/ppermute | solution.py:195
  20.2 12.2 %collective-permute-start.3 = (bf16[512,256]{1,0:T(8,128)(2,1)S(1)}, bf16[512,256]{1,0:T(8,128)(2,1)S(1)}, u32[]{:S(2)}, u32[]{:S(2)}) collective-permute-start(bf16[512,256]{1,0:T(8,128)(2,1)S(1)} %get-tuple-element.55), channel_id=1, source_target_pairs={{0,4},{2,6},{4,8},{6,10},{8,12},{10,14},{12,16},{14,18},{16,20},{1... | collective-permute-start | bytes 786440 | tf_op jit(solution)/shard_map/ppermute | solution.py:187
  25.4 7.8 %collective-permute-start.7 = (bf16[512,256]{1,0:T(8,128)(2,1)S(1)}, bf16[512,256]{1,0:T(8,128)(2,1)S(1)}, u32[]{:S(2)}, u32[]{:S(2)}) collective-permute-start(bf16[512,256]{1,0:T(8,128)(2,1)S(1)} %get-tuple-element.58), channel_id=1, source_target_pairs={{0,2},{2,0},{4,6},{6,4},{8,10},{10,8},{12,14},{14,12},{16,18},{18,... | collective-permute-start | bytes 786440 | tf_op jit(solution)/shard_map/ppermute | solution.py:202
  25.9 14.6 %collective-permute-start.2 = (bf16[512,256]{1,0:T(8,128)(2,1)S(1)}, bf16[512,256]{1,0:T(8,128)(2,1)S(1)}, u32[]{:S(2)}, u32[]{:S(2)}) collective-permute-start(bf16[512,256]{1,0:T(8,128)(2,1)S(1)} %get-tuple-element.53), channel_id=1, source_target_pairs={{0,4},{2,6},{4,8},{6,10},{8,12},{10,14},{12,16},{14,18},{16,20},{1... | collective-permute-start | bytes 786440 | tf_op jit(solution)/shard_map/ppermute | solution.py:187
  25.9 21.6 %collective-permute-start.10 = (bf16[512,256]{1,0:T(8,128)(2,1)S(1)}, bf16[512,256]{1,0:T(8,128)(2,1)S(1)}, u32[]{:S(2)}, u32[]{:S(2)}) collective-permute-start(bf16[512,256]{1,0:T(8,128)(2,1)S(1)} %get-tuple-element.68), channel_id=1, source_target_pairs={{0,4},{2,6},{4,8},{6,10},{8,12},{10,14},{12,16},{14,18},{16,20},{1... | collective-permute-start | bytes 786440 | tf_op jit(solution)/shard_map/ppermute | solution.py:187
  32.4 3.7 %collective-permute-start.6 = (bf16[512,256]{1,0:T(8,128)(2,1)S(1)}, bf16[512,256]{1,0:T(8,128)(2,1)S(1)}, u32[]{:S(2)}, u32[]{:S(2)}) collective-permute-start(bf16[512,256]{1,0:T(8,128)(2,1)S(1)} %collective-permute-done.3.far2), channel_id=1, source_target_pairs={{0,2},{2,0},{4,6},{6,4},{8,10},{10,8},{12,14},{14,12},{16,18},{18,... | collective-permute-start | bytes 786440 | tf_op jit(solution)/shard_map/ppermute | solution.py:195
  33.2 2.9 %copy-start.2 = (bf16[512,1024]{1,0:T(8,128)(2,1)S(1)}, bf16[512,1024]{1,0:T(8,128)(2,1)}, u32[]{:S(2)}) copy-start(bf16[512,1024]{1,0:T(8,128)(2,1)} %get-tuple-element.54.heads) | copy-start | bytes 3145732
  33.4 16.6 %collective-permute-start.13 = (bf16[512,256]{1,0:T(8,128)(2,1)S(1)}, bf16[512,256]{1,0:T(8,128)(2,1)S(1)}, u32[]{:S(2)}, u32[]{:S(2)}) collective-permute-start(bf16[512,256]{1,0:T(8,128)(2,1)S(1)} %get-tuple-element.107), channel_id=1, source_target_pairs={{0,1},{1,0},{2,3},{3,2},{4,5},{5,4},{6,7},{7,6},{8,9},{9,8},{10,11... | collective-permute-start | bytes 786440 | tf_op jit(solution)/shard_map/ppermute | solution.py:207
  40.1 1.6 %collective-permute-start.9 = (bf16[512,256]{1,0:T(8,128)(2,1)S(1)}, bf16[512,256]{1,0:T(8,128)(2,1)S(1)}, u32[]{:S(2)}, u32[]{:S(2)}) collective-permute-start(bf16[512,256]{1,0:T(8,128)(2,1)S(1)} %get-tuple-element.62), channel_id=1, source_target_pairs={{0,2},{2,0},{4,6},{6,4},{8,10},{10,8},{12,14},{14,12},{16,18},{18,... | collective-permute-start | bytes 786440 | tf_op jit(solution)/shard_map/ppermute | solution.py:202
  40.5 2.3 %collective-permute-start.8 = (bf16[512,256]{1,0:T(8,128)(2,1)S(1)}, bf16[512,256]{1,0:T(8,128)(2,1)S(1)}, u32[]{:S(2)}, u32[]{:S(2)}) collective-permute-start(bf16[512,256]{1,0:T(8,128)(2,1)S(1)} %collective-permute-done.2.far2), channel_id=1, source_target_pairs={{0,2},{2,0},{4,6},{6,4},{8,10},{10,8},{12,14},{14,12},{16,18},{18,... | collective-permute-start | bytes 786440 | tf_op jit(solution)/shard_map/ppermute | solution.py:195
  40.8 2.0 %copy-start.1 = (bf16[512,1024]{1,0:T(8,128)(2,1)S(1)}, bf16[512,1024]{1,0:T(8,128)(2,1)}, u32[]{:S(2)}) copy-start(bf16[512,1024]{1,0:T(8,128)(2,1)} %get-tuple-element.52.heads) | copy-start | bytes 3145732
  41.9 14.4 %collective-permute-start.17 = (bf16[512,256]{1,0:T(8,128)(2,1)S(1)}, bf16[512,256]{1,0:T(8,128)(2,1)S(1)}, u32[]{:S(2)}, u32[]{:S(2)}) collective-permute-start(bf16[512,256]{1,0:T(8,128)(2,1)S(1)} %get-tuple-element.109), channel_id=1, source_target_pairs={{0,1},{1,0},{2,3},{3,2},{4,5},{5,4},{6,7},{7,6},{8,9},{9,8},{10,11... | collective-permute-start | bytes 786440 | tf_op jit(solution)/shard_map/ppermute | solution.py:207
  46.8 3.2 %collective-permute-start.12 = (bf16[512,256]{1,0:T(8,128)(2,1)S(1)}, bf16[512,256]{1,0:T(8,128)(2,1)S(1)}, u32[]{:S(2)}, u32[]{:S(2)}) collective-permute-start(bf16[512,256]{1,0:T(8,128)(2,1)S(1)} %get-tuple-element.69), channel_id=1, source_target_pairs={{0,2},{2,0},{4,6},{6,4},{8,10},{10,8},{12,14},{14,12},{16,18},{18,... | collective-permute-start | bytes 786440 | tf_op jit(solution)/shard_map/ppermute | solution.py:202
  47.5 3.0 %collective-permute-start.11 = (bf16[512,256]{1,0:T(8,128)(2,1)S(1)}, bf16[512,256]{1,0:T(8,128)(2,1)S(1)}, u32[]{:S(2)}, u32[]{:S(2)}) collective-permute-start(bf16[512,256]{1,0:T(8,128)(2,1)S(1)} %collective-permute-done.10.far2), channel_id=1, source_target_pairs={{0,2},{2,0},{4,6},{6,4},{8,10},{10,8},{12,14},{14,12},{16,18},{18,... | collective-permute-start | bytes 786440 | tf_op jit(solution)/shard_map/ppermute | solution.py:195
  47.6 15.3 %collective-permute-start.15 = (bf16[2,512,256]{2,1,0:T(8,128)(2,1)S(1)}, bf16[2,512,256]{2,1,0:T(8,128)(2,1)S(1)}, u32[]{:S(2)}, u32[]{:S(2)}) collective-permute-start(bf16[2,512,256]{2,1,0:T(8,128)(2,1)S(1)} %pad_maximum_fusion.2), channel_id=1, source_target_pairs={{0,1},{1,0},{2,3},{3,2},{4,5},{5,4},{6,7},{7,6},{8,9},{9,8},{10,11... | collective-permute-start | bytes 1572872 | tf_op jit(solution)/shard_map/ppermute | solution.py:211
  50.0 1.2 %copy-start = (bf16[512,1024]{1,0:T(8,128)(2,1)S(1)}, bf16[512,1024]{1,0:T(8,128)(2,1)}, u32[]{:S(2)}) copy-start(bf16[512,1024]{1,0:T(8,128)(2,1)} %get-tuple-element.67.heads) | copy-start | bytes 3145732
  50.2 12.8 %collective-permute-start.16 = (bf16[512,256]{1,0:T(8,128)(2,1)S(1)}, bf16[512,256]{1,0:T(8,128)(2,1)S(1)}, u32[]{:S(2)}, u32[]{:S(2)}) collective-permute-start(bf16[512,256]{1,0:T(8,128)(2,1)S(1)} %get-tuple-element.111), channel_id=1, source_target_pairs={{4,0},{6,2},{8,4},{10,6},{12,8},{14,10},{16,12},{18,14},{20,16},{2... | collective-permute-start | bytes 786440 | tf_op jit(solution)/shard_map/ppermute | solution.py:210
  55.2 1.9 %collective-permute-start.14 = (bf16[512,256]{1,0:T(8,128)(2,1)S(1)}, bf16[512,256]{1,0:T(8,128)(2,1)S(1)}, u32[]{:S(2)}, u32[]{:S(2)}) collective-permute-start(bf16[512,256]{1,0:T(8,128)(2,1)S(1)} %get-tuple-element.90), channel_id=1, source_target_pairs={{0,2},{2,0},{4,6},{6,4},{8,10},{10,8},{12,14},{14,12},{16,18},{18,... | collective-permute-start | bytes 786440 | tf_op jit(solution)/shard_map/ppermute | solution.py:202
  57.3 7.6 %collective-permute-start.18 = (bf16[512,256]{1,0:T(8,128)(2,1)S(1)}, bf16[512,256]{1,0:T(8,128)(2,1)S(1)}, u32[]{:S(2)}, u32[]{:S(2)}) collective-permute-start(bf16[512,256]{1,0:T(8,128)(2,1)S(1)} %get-tuple-element.104), channel_id=1, source_target_pairs={{4,0},{6,2},{8,4},{10,6},{12,8},{14,10},{16,12},{18,14},{20,16},{2... | collective-permute-start | bytes 786440 | tf_op jit(solution)/shard_map/ppermute | solution.py:210
